TPU v7x, 128 devices: a whole 4x4x4 slice. The times are simulated.
128 devices in a mesh: group: 8 (over y, core), seq: 16 (over z, x).
Axes of the slice: x: 4, y: 4, z: 4, core: 2. Of those that a mesh axis runs over, the one named last changes fastest.
Arguments:
- query: bfloat16 [16384, 12288], P(('group', 'seq')), may hold values from -210 to 210, as said below
- latent_raw: bfloat16 [16384, 512], P(('group', 'seq')), may hold values from -6 to 6
- rope_raw: bfloat16 [16384, 64], P(('group', 'seq')), may hold values from -6 to 6
- kv_gain: float32 [512], replicated, may hold values from 0.1 to 1.9
- w_uk: bfloat16 [512, 8192], replicated, may hold values from -0.25 to 0.25
- w_uv: bfloat16 [512, 8192], replicated, may hold values from -0.25 to 0.25
- request_lengths: int32 [8, 32], P('group'), may hold values from 1 to 128, 2048 in all within a row
- page_owner: int32 [256], replicated, may hold values from 0 to 127, as said below
- page_slot: int32 [256], replicated, may hold values from 0 to 3, as said below
Outputs:
- attended: bfloat16 [16384, 8192], P(('group', 'seq'))
- decode_cache: bfloat16 [512, 36864], P(('group', 'seq'))
Inputs may be any that keep to these rules, and one draw needn't show every extreme that they name: `request_lengths`: each row sums to 2048; no request is longer than 128 tokens. `query`: large rows may occur. `page_owner`: no owner gets more than 4 pages, and some owner gets exactly 4. `page_slot`: pages of one owner have distinct slots.
All inputs are finite; a program needn't handle non-finite values.
Results may differ from a plain program's by a relative error of at most 0.012.
The roundings to bfloat16 on the way count: a program that leaves them out, or rounds other values in their place, can miss the bound.
Values may be sent and summed in bfloat16 or wider, within the bound.
A program may use at most 192 MiB of HBM per device.

v0:
```python
import jax
import jax.numpy as jnp
from jax import lax
from jax.sharding import PartitionSpec as P

HEADS = 64
NOPE = 128
ROPE = 64
VDIM = 128
PAGE_TOK = 64


def passed_along(x, axis, by):
    devices = lax.axis_size(axis)
    pairs = [(i, i + by) for i in range(devices) if 0 <= i + by < devices]
    return lax.ppermute(x, axis, pairs)


def request_info(lengths, index):
    starts = jnp.cumsum(lengths) - lengths
    inside = starts[None, :] <= index[:, None]
    rid = jnp.sum(inside.astype(jnp.int32), axis=1) - 1
    begin = jnp.max(jnp.where(inside, starts[None, :], 0), axis=1)
    return (rid, index - begin)


def rotary(values, position):
    half = values.shape[-1] // 2
    freqs = 10000.0 ** (-jnp.arange(half, dtype=jnp.float32) / half)
    angle = position.astype(jnp.float32)[:, None] * freqs[None, :]
    shape = (values.shape[0],) + (1,) * (values.ndim - 2) + (half,)
    cosine = jnp.cos(angle).reshape(shape)
    sine = jnp.sin(angle).reshape(shape)
    first = values[..., :half]
    second = values[..., half:]
    return jnp.concatenate([first * cosine - second * sine, second * cosine + first * sine], -1)


def on_device(
    query, latent_raw, rope_raw, kv_gain, w_uk, w_uv, request_lengths, page_owner, page_slot
):
    count = latent_raw.shape[0]
    seq_count = lax.axis_size("seq")
    group_count = lax.axis_size("group")
    seq_here = lax.axis_index("seq")
    group_here = lax.axis_index("group")
    lengths = request_lengths[0]
    own_index = seq_here * count + jnp.arange(count, dtype=jnp.int32)
    prev_index = own_index - count
    rid_own, pos_own = request_info(lengths, own_index)
    rid_prev, unused_pos = request_info(lengths, prev_index)
    source = latent_raw.astype(jnp.float32)
    scale_norm = lax.rsqrt(jnp.mean(source * source, axis=1, keepdims=True) + 1e-06)
    latent = (source * scale_norm * kv_gain[None, :]).astype(jnp.bfloat16)
    key_rope = rotary(rope_raw.astype(jnp.float32), pos_own).astype(jnp.bfloat16)
    key_own = jnp.dot(latent, w_uk, preferred_element_type=jnp.float32).astype(jnp.bfloat16)
    value_own = jnp.dot(latent, w_uv, preferred_element_type=jnp.float32).astype(jnp.bfloat16)
    key_prev, value_prev, rope_prev = passed_along((key_own, value_own, key_rope), "seq", 1)
    keys = jnp.concatenate([key_prev, key_own], axis=0).reshape(2 * count, HEADS, NOPE)
    values = jnp.concatenate([value_prev, value_own], axis=0).reshape(2 * count, HEADS, VDIM)
    ropes = jnp.concatenate([rope_prev, key_rope], axis=0)
    rid_keys = jnp.concatenate([rid_prev, rid_own], axis=0)
    key_index = jnp.concatenate([prev_index, own_index], axis=0)
    shaped = query.reshape(count, HEADS, NOPE + ROPE)
    query_nope = shaped[:, :, :NOPE]
    query_rope = rotary(shaped[:, :, NOPE:].astype(jnp.float32), pos_own).astype(jnp.bfloat16)
    factor = 1.0 / (NOPE + ROPE) ** 0.5
    allowed = (rid_own[:, None] == rid_keys[None, :]) & (key_index[None, :] <= own_index[:, None])
    score = jnp.einsum("thd,uhd->thu", query_nope, keys, preferred_element_type=jnp.float32)
    score = score + jnp.einsum("thd,ud->thu", query_rope, ropes, preferred_element_type=jnp.float32)
    score = jnp.where(allowed[:, None, :], score * factor, -1e30)
    top = jnp.max(score, axis=2, keepdims=True)
    weights = jnp.where(allowed[:, None, :], jnp.exp(score - top), 0.0)
    probs = (weights / jnp.sum(weights, axis=2, keepdims=True)).astype(jnp.bfloat16)
    attended = jnp.einsum("thu,uhd->thd", probs, values, preferred_element_type=jnp.float32)
    attended = attended.astype(jnp.bfloat16).reshape(count, HEADS * VDIM)
    pages_dev = count // PAGE_TOK
    slots = 2 * pages_dev
    rows = jnp.concatenate([latent, key_rope], axis=1).reshape(pages_dev, -1)
    width = rows.shape[1]
    owner_here = group_here * seq_count + seq_here
    slot_ids = jnp.arange(slots, dtype=jnp.int32)
    owners_total = group_count * seq_count
    my_pages = owner_here * pages_dev + jnp.arange(pages_dev, dtype=jnp.int32)
    dest = page_owner[my_pages]
    hit = dest[None, :] == jnp.arange(owners_total, dtype=jnp.int32)[:, None]
    outgoing = jnp.where(hit[:, :, None], rows[None, :, :], jnp.zeros((), jnp.bfloat16))
    arrived = lax.all_to_all(outgoing, ("group", "seq"), split_axis=0, concat_axis=0, tiled=True)
    flat = arrived.reshape(-1, width)
    pick = ((page_owner[None, :] == owner_here) & (page_slot[None, :] == slot_ids[:, None])).astype(
        jnp.bfloat16
    )
    cache = jnp.dot(pick, flat, preferred_element_type=jnp.float32).astype(jnp.bfloat16)
    return (attended, cache)


def solution(mesh):
    placed = (
        P(("group", "seq"), None),
        P(("group", "seq"), None),
        P(("group", "seq"), None),
        P(),
        P(),
        P(),
        P("group", None),
        P(),
        P(),
    )
    return jax.shard_map(
        on_device,
        mesh=mesh,
        in_specs=placed,
        out_specs=(P(("group", "seq"), None), P(("group", "seq"), None)),
        check_vma=False,
    )
```

profile of v0, /device:TPU:74, one launch (start us, length us, event | category | flops | bytes accessed | tf_op | source)
XLA Modules:
  0.0 476.4 jit_solution(15741270586240675904)
XLA Ops:
  0.7 1.0 fusion.12
  1.7 0.9 reduce-window_clone.1
  3.2 1.3 gather_fusion
  4.6 0.7 convert_element_type.55
  5.8 1.0 fusion.14
  7.1 16.7 %broadcast_select_fusion = bf16[128,2,36864]{2,1,0:T(2,128)(2,1)} fusion(pred[128,2]{1,0:T(8,128)(4,1)S(1)} %iota_compare_fusion, bf16[2,36864]{1,0:T(2,128)(2,1)S(1)} %broadcast_in_dim.55), kind=kLoop, calls=%fused_computation.3 | loop fusion | flops 9437184 | bytes 19022080 | tf_op jit(solution)/shard_map/jit(_where)/select_n | solution.py:87
  23.9 10.4 %all-to-all-start = ((bf16[128,2,36864]{2,1,0:T(2,128)(2,1)}), bf16[128,2,36864]{2,1,0:T(2,128)(2,1)}, u32[]{:S(2)}, u32[]{:S(2)}) async-start(bf16[128,2,36864]{2,1,0:T(2,128)(2,1)} %broadcast_select_fusion), calls=%async_computation | async-start | bytes 37748736 | tf_op jit(solution)/shard_map/all_to_all | solution.py:88
  34.3 6.0 %convolution_convert_fusion.2 = bf16[128,8192]{1,0:T(8,128)(2,1)} fusion(bf16[128,512]{1,0:T(8,128)(2,1)S(1)} %fusion.14, bf16[512,8192]{1,0:T(8,128)(2,1)} %param.14), kind=kOutput, calls=%fused_computation.5 | convolution fusion | flops 1074790400 | bytes 10616832 | tf_op jit(solution)/shard_map/dot_general | solution.py:57
  40.2 3.4 collective-permute-start
  43.6 3.1 collective-permute-start.2
  46.7 6.0 %convolution_convert_fusion.1 = bf16[128,8192]{1,0:T(8,128)(2,1)} fusion(bf16[128,512]{1,0:T(8,128)(2,1)S(1)} %fusion.14, bf16[512,8192]{1,0:T(8,128)(2,1)} %param.13), kind=kOutput, calls=%fused_computation.4 | convolution fusion | flops 1074790400 | bytes 10616832 | tf_op jit(solution)/shard_map/dot_general | solution.py:56
  52.7 3.6 collective-permute-start.1
  56.3 3.5 copy.59
  60.2 1.3 subtract_convert_fusion
  61.5 304.4 %collective-permute-done = bf16[128,8192]{1,0:T(8,128)(2,1)} collective-permute-done((bf16[128,8192]{1,0:T(8,128)(2,1)}, bf16[128,8192]{1,0:T(8,128)(2,1)}, u32[]{:S(2)}, u32[]{:S(2)}) %collective-permute-start) | collective-permute-done | bytes 2097184 | tf_op jit(solution)/shard_map/ppermute | solution.py:16
  365.9 4.6 pad_maximum_fusion
  370.5 40.2 %collective-permute-done.1 = bf16[128,8192]{1,0:T(8,128)(2,1)} collective-permute-done((bf16[128,8192]{1,0:T(8,128)(2,1)}, bf16[128,8192]{1,0:T(8,128)(2,1)}, u32[]{:S(2)}, u32[]{:S(2)}) %collective-permute-start.1) | collective-permute-done | bytes 2097184 | tf_op jit(solution)/shard_map/ppermute | solution.py:16
  410.7 6.7 %fusion.3 = f32[64,256,128]{2,1,0:T(8,128)} fusion(bf16[128,64,192]{0,2,1:T(8,128)(2,1)S(1)} %bitcast.36, bf16[128,8192]{1,0:T(8,128)(2,1)} %convolution_convert_fusion.1, bf16[128,8192]{1,0:T(8,128)(2,1)} %collective-permute-done.1), kind=kOutput, calls=%fused_computation.11 | convolution fusion | flops 545259520 | bytes 14680064 | tf_op jit(solution)/shard_map/thd,uhd->thu/dot_general | solution.py:69
  417.4 6.5 %copy.70 = bf16[256,8192]{0,1:T(8,128)(2,1)} copy(bf16[256,8192]{1,0:T(8,128)(2,1)} %pad_maximum_fusion) | data formatting | bytes 8388608 | tf_op jit(solution)/shard_map/reshape | solution.py:60
  423.9 7.8 %fusion.27 = (f32[128,64]{0,1:T(8,128)S(1)}, f32[128,64,256]{0,2,1:T(8,128)}) fusion(pred[128,256]{0,1:T(8,128)(4,1)S(1)} %compare_and_fusion, f32[64,256,128]{2,1,0:T(8,128)} %fusion.3, bf16[128,64,32]{0,2,1:T(8,128)(2,1)S(1)} %copy-done.2, bf16[128,64,32]{0,2,1:T(8,128)(2,1)S(1)} %copy-done.1, bf16[128,32]{0,1:T(8,128)(2,1)S(1)} %get-tuple-element.20, ...), kind=kOutput, calls=%fused_computation.67 | convolution fusion | flops 283214080 | bytes 17924096 | tf_op jit(solution)/shard_map/sub | solution.py:73
  431.7 5.9 %fusion.8 = bf16[64,128,128]{2,1,0:T(8,128)(2,1)S(1)} fusion(bf16[256,64,128]{0,2,1:T(8,128)(2,1)} %bitcast.37, f32[128,64,256]{0,2,1:T(8,128)} %get-tuple-element.24, f32[128,64]{0,1:T(8,128)S(1)} %get-tuple-element.23), kind=kOutput, calls=%fused_computation.18 | convolution fusion | flops 542113792 | bytes 14712832 | tf_op jit(solution)/shard_map/thu,uhd->thd/dot_general | solution.py:75
  437.6 2.9 copy.67
  440.5 26.3 %reshape.196 = bf16[256,36864]{1,0:T(8,128)(2,1)} reshape(bf16[128,2,36864]{2,1,0:T(2,128)(2,1)} %all-to-all-done) | data formatting | bytes 37748736 | tf_op jit(solution)/shard_map/reshape | solution.py:89
  466.8 9.6 %convolution_convert_fusion = bf16[4,36864]{1,0:T(4,128)(2,1)} fusion(bf16[256,36864]{1,0:T(8,128)(2,1)} %reshape.196, s32[256]{0:T(256)S(1)} %copy-done.3, pred[256]{0:T(512)(128)(4,1)S(1)} %broadcast_compare_fusion), kind=kOutput, calls=%fused_computation.2 | convolution fusion | flops 75646976 | bytes 19170560 | tf_op jit(solution)/shard_map/dot_general | solution.py:93
  (32 shorter events, 1.9 us)
Async XLA Ops:
  23.9 416.6 %all-to-all-start = ((bf16[128,2,36864]{2,1,0:T(2,128)(2,1)}), bf16[128,2,36864]{2,1,0:T(2,128)(2,1)}, u32[]{:S(2)}, u32[]{:S(2)}) async-start(bf16[128,2,36864]{2,1,0:T(2,128)(2,1)} %broadcast_select_fusion), calls=%async_computation | async-start | bytes 37748736 | tf_op jit(solution)/shard_map/all_to_all | solution.py:88
  40.2 325.7 %collective-permute-start = (bf16[128,8192]{1,0:T(8,128)(2,1)}, bf16[128,8192]{1,0:T(8,128)(2,1)}, u32[]{:S(2)}, u32[]{:S(2)}) collective-permute-start(bf16[128,8192]{1,0:T(8,128)(2,1)} %convolution_convert_fusion.2), channel_id=1, source_target_pairs={{0,1},{1,2},{2,3},{3,4},{4,5},{5,6},{6,7},{7,8},{8,9},{9,10},{10,1... | collective-permute-start | bytes 6291464 | tf_op jit(solution)/shard_map/ppermute | solution.py:16
  43.6 380.2 %collective-permute-start.2 = (bf16[128,64]{0,1:T(8,128)(2,1)S(1)}, bf16[128,64]{0,1:T(8,128)(2,1)S(1)}, u32[]{:S(2)}, u32[]{:S(2)}) collective-permute-start(bf16[128,64]{0,1:T(8,128)(2,1)S(1)} %pad_maximum_fusion.2), channel_id=1, source_target_pairs={{0,1},{1,2},{2,3},{3,4},{4,5},{5,6},{6,7},{7,8},{8,9},{9,10},{10,1... | collective-permute-start | bytes 49160 | tf_op jit(solution)/shard_map/ppermute | solution.py:16
  52.7 7.1 %copy-start = (s32[256]{0:T(256)S(1)}, s32[256]{0:T(256)}, u32[]{:S(2)}) copy-start(s32[256]{0:T(256)} %param.16) | copy-start | bytes 3076
  52.7 358.0 %collective-permute-start.1 = (bf16[128,8192]{1,0:T(8,128)(2,1)}, bf16[128,8192]{1,0:T(8,128)(2,1)}, u32[]{:S(2)}, u32[]{:S(2)}) collective-permute-start(bf16[128,8192]{1,0:T(8,128)(2,1)} %convolution_convert_fusion.1), channel_id=1, source_target_pairs={{0,1},{1,2},{2,3},{3,4},{4,5},{5,6},{6,7},{7,8},{8,9},{9,10},{10,1... | collective-permute-start | bytes 6291464 | tf_op jit(solution)/shard_map/ppermute | solution.py:16
  417.4 6.5 %copy-start.1 = (bf16[128,64,32]{0,2,1:T(8,128)(2,1)S(1)}, bf16[128,64,32]{0,2,1:T(8,128)(2,1)}, u32[]{:S(2)}) copy-start(bf16[128,64,32]{0,2,1:T(8,128)(2,1)} %get-tuple-element.17) | copy-start | bytes 1572868
  417.4 6.5 %copy-start.2 = (bf16[128,64,32]{0,2,1:T(8,128)(2,1)S(1)}, bf16[128,64,32]{0,2,1:T(8,128)(2,1)}, u32[]{:S(2)}) copy-start(bf16[128,64,32]{0,2,1:T(8,128)(2,1)} %get-tuple-element.18) | copy-start | bytes 1572868
  440.5 26.3 %copy-start.3 = (s32[256]{0:T(256)S(1)}, s32[256]{0:T(256)}, u32[]{:S(2)}) copy-start(s32[256]{0:T(256)} %param.17) | copy-start | bytes 3076
where the time goes:
time: 478 us; the launch traced here: 476 us
  waiting for transfers between devices  345 us (72%)
  matrix products  42 us (9%)
  local copies, waits for them, and re-layouts  40.9 us (9%)
  other arithmetic  27.7 us (6%)
  starting transfers between devices  20.4 us (4%)
    ppermute x3, waiting for transfers between devices, passed_along(): return lax.ppermute(x, axis, pairs)  345 us
    reshape x1, local copies, waits for them, and re-layouts, on_device(): flat = arrived.reshape(-1, width)  26.3 us
    select_n x1, other arithmetic, on_device(): jnp.where(hit[:, :, None], rows[None, :, :], jnp.zeros((), jnp.bfloat16))  16.7 us
    all_to_all x1, starting transfers between devices, on_device(): lax.all_to_all(outgoing, ('group', 'seq'), split_axis=0, concat_axis=0, t...  10.4 us
    ppermute x3, starting transfers between devices, passed_along(): return lax.ppermute(x, axis, pairs)  10.1 us
    dot_general x1, matrix products, on_device(): jnp.dot(pick, flat, preferred_element_type=jnp.float32).astype(jnp.bfloat16)  9.63 us
  transfers between devices with their start and end apart: 4, of which 2 were waited for; matrix products, arithmetic and copies ran while one was open for 11% of the time, Pallas kernels for 0%

commit v1 on v0

v1 whole, which is shorter than its diff:
```python
import functools

import jax
import jax.numpy as jnp
import numpy as np
from jax import lax
from jax.experimental import pallas as pl
from jax.experimental.pallas import tpu as pltpu
from jax.sharding import PartitionSpec as P
import ml_dtypes

MESH = pl.DeviceIdType.MESH
F32 = jnp.float32
BF16 = jnp.bfloat16
TOK = 128
HEADS = 64
LATENT = 512
QUADS = 16
TILES = 5
CHUNKS = QUADS * TILES
STEPS = 16
FIRST = 11
PAGE_W = 36864
SCALE = float(1.0 / 192.0**0.5 * np.log2(np.e))


def trig_table():
    freqs = (10000.0 ** (-np.arange(32, dtype=np.float64) / 32.0)).astype(np.float32)
    angle = np.arange(TOK, dtype=np.float32)[:, None] * freqs[None, :]
    cosine = np.cos(angle.astype(np.float64)).astype(np.float32)
    sine = np.sin(angle.astype(np.float64)).astype(np.float32)
    full = np.concatenate([cosine] * 4 + [-sine, sine, -sine, sine], axis=1)
    parts = []
    for _ in range(3):
        part = full.astype(ml_dtypes.bfloat16)
        parts.append(part)
        full = full - part.astype(np.float32)
    return np.concatenate(parts, axis=0)


def middle_of(quad, tile):
    if tile < 4:
        return (2 * tile, quad)
    return (2 * ((8 - quad // 4 - quad % 4) % 4) + 1, quad)


def remote(src, dst, send, recv, device):
    return pltpu.make_async_remote_copy(
        src_ref=src, dst_ref=dst, send_sem=send, recv_sem=recv, device_id=device, device_id_type=MESH
    )


def done(ref, sem):
    pltpu.make_async_copy(ref, ref, sem).wait()


def rotated(x, cosine, sine, low):
    partner = jnp.where(low, pltpu.roll(x, 96, 1), pltpu.roll(x, 32, 1))
    return x * cosine + partner * sine


def kernel(
    lengths, latent_raw, rope_raw, gain, owner, slot, trig, query, w_uk, w_uv,
    out, cache,
    qv, kv, vv, ov, lat2, kr2, krh, cos_v, sin_v, bias, ypage, xs, rs, rf, of, os, cb, cf, cout, onehot,
    q_sem, k_sem, v_sem, o_sem, send_n, recv_n, send1, recv1, send2, recv2, c_sem,
):
    g, s = lax.axis_index("group"), lax.axis_index("seq")
    me = g * 16 + s
    core, y = g % 2, g // 2
    diagonal = (s // 4 + s % 4 + y) % 4 == 0
    middle = (core == 0) | diagonal
    my_tile = jnp.where(core == 0, y, 4)
    my_chunk = s * TILES + my_tile
    has_left, has_right = s > 0, s < 15

    barrier = pltpu.get_barrier_semaphore()

    def greet(device):
        pl.semaphore_signal(barrier, inc=1, device_id=device, device_id_type=MESH)

    @pl.when(middle)
    def _():
        for quad in range(QUADS):
            for row in range(4):
                if (quad // 4 + quad % 4 + row) % 4 != 0:
                    greet((2 * row + 1, quad))

    def each_middle(act):
        for step in range(QUADS):
            quad = (s + step) % 16
            for tile in range(TILES):
                device = middle_of(quad, tile)
                if step:
                    act(quad, tile, device)
                else:
                    pl.when(device[0] != g)(functools.partial(act, quad, tile, device))

    each_middle(lambda quad, tile, device: greet(device))

    @pl.when(has_left)
    def _():
        greet((g, s - 1))

    def fetches(i):
        return (
            pltpu.make_async_copy(query.at[:, pl.ds(i * 768, 768)], qv.at[i], q_sem.at[i]),
            pltpu.make_async_copy(w_uk.at[:, pl.ds(i * 512, 512)], kv.at[i], k_sem.at[i]),
            pltpu.make_async_copy(w_uv.at[:, pl.ds(i * 512, 512)], vv.at[i], v_sem.at[i]),
        )

    for i in range(STEPS):
        for fetch in fetches(i):
            fetch.start()

    row = lax.broadcasted_iota(jnp.int32, (TOK, TOK), 0)
    col = lax.broadcasted_iota(jnp.int32, (TOK, TOK), 1)
    low = col % 64 < 32
    half = col < 64
    index = row + s * TOK
    begin = jnp.zeros((TOK, TOK), jnp.int32)
    start = jnp.int32(0)
    for r in range(32):
        begin = jnp.where(index >= start, start, begin)
        start = start + lengths[0, r]
    pos = index - begin
    hot = (col == pos).astype(F32).astype(BF16)
    angles = jnp.dot(jnp.concatenate([hot, hot, hot], axis=1), trig[...], preferred_element_type=F32)
    cosine, sine = angles[:, :TOK], angles[:, TOK:]
    cos_v[...] = cosine
    sin_v[...] = sine
    bias[...] = jnp.where((row - col + TOK) % TOK <= pos, 0.0, -1e30)

    source = latent_raw[...].astype(F32)
    norm = lax.rsqrt(jnp.mean(source * source, axis=1, keepdims=True) + 1e-06)
    latent = (source * norm * gain[...]).astype(BF16)
    lat2[TOK:, :] = latent
    rope = rope_raw[...].astype(F32)
    key_rope = rotated(jnp.concatenate([rope, rope], axis=1), cosine, sine, low).astype(BF16)
    kr2[TOK:, :] = key_rope

    wide, tail = latent.astype(F32), key_rope.astype(F32)
    plain = [wide[:, i * 128 : (i + 1) * 128] for i in range(4)]
    turned = [pltpu.roll(x, 64, 1) for x in plain]
    moved = (
        [turned[0]]
        + [jnp.where(half, turned[i - 1], turned[i]) for i in range(1, 4)]
        + [jnp.where(half, turned[3], tail)]
    )
    odd = row % 2 == 1
    upper = lax.broadcasted_iota(jnp.int32, (8, 128), 0) < 4
    for tile, (a, b) in enumerate(zip(plain + [tail], moved)):
        ypage[tile] = jnp.where(odd, b, a)
    for tile in range(TILES):
        for octet in range(8):
            first = ypage[tile, octet * 8 : octet * 8 + 8, :]
            second = ypage[tile, 64 + octet * 8 : 64 + octet * 8 + 8, :]
            xs[2 * octet * TILES + tile] = jnp.where(upper, first, pltpu.roll(second, 4, 0)).astype(BF16)
            xs[(2 * octet + 1) * TILES + tile] = jnp.where(upper, pltpu.roll(first, 4, 0), second).astype(BF16)

    pl.semaphore_wait(barrier, jnp.where(middle, 127, CHUNKS) + jnp.where(has_right, 1, 0))

    lat_copy = remote(lat2.at[pl.ds(TOK, TOK)], lat2.at[pl.ds(0, TOK)], send_n.at[0], recv_n.at[0], (g, s + 1))
    rope_copy = remote(kr2.at[pl.ds(TOK, TOK)], kr2.at[pl.ds(0, TOK)], send_n.at[1], recv_n.at[1], (g, s + 1))

    @pl.when(has_right)
    def _():
        lat_copy.start()
        rope_copy.start()

    each_middle(
        lambda quad, tile, device: remote(xs.at[quad * TILES + tile], rs.at[me], send1, recv1, device).start()
    )

    @pl.when(middle)
    def _():
        rs[me] = xs[my_chunk]
        want = slot[...] * 128 + owner[...]
        onehot[...] = (lax.broadcasted_iota(jnp.int32, (512, 256), 0) == want).astype(F32).astype(BF16)

    @pl.when(has_left)
    def _():
        done(lat2.at[pl.ds(0, TOK)], recv_n.at[0])
        done(kr2.at[pl.ds(0, TOK)], recv_n.at[1])

    @pl.when(s == 0)
    def _():
        lat2[:TOK, :] = jnp.zeros((TOK, LATENT), BF16)
        kr2[:TOK, :] = jnp.zeros((TOK, TOK), BF16)

    half2 = lax.broadcasted_iota(jnp.int32, (2 * TOK, TOK), 1) < 64
    ropes = kr2[...].astype(F32)
    krh[0] = jnp.where(half2, ropes, 0.0).astype(BF16)
    krh[1] = jnp.where(half2, 0.0, ropes).astype(BF16)

    def attend(i):
        for fetch in fetches(i):
            fetch.wait()
        keys = jnp.dot(lat2[...], kv[i], preferred_element_type=F32).astype(BF16)
        values = jnp.dot(lat2[...], vv[i], preferred_element_type=F32).astype(BF16)
        row = lax.broadcasted_iota(jnp.int32, (TOK, TOK), 0)
        col = lax.broadcasted_iota(jnp.int32, (TOK, TOK), 1)
        own = col <= row
        half = col < 64
        low = col % 64 < 32
        for pair in range(2):
            tiles = [qv[i, :, pl.ds(pair * 384 + t * 128, 128)].astype(F32) for t in range(3)]
            turn = rotated(jnp.where(half, tiles[1], tiles[2]), cos_v[...], sin_v[...], low).astype(BF16)
            second = pltpu.roll(jnp.where(half, tiles[2], tiles[1]), 64, 1).astype(BF16)
            for one, nope in enumerate((tiles[0].astype(BF16), second)):
                h = 2 * pair + one
                left = jnp.concatenate([nope, turn], axis=1)
                right = jnp.concatenate([keys[:, h * 128 : (h + 1) * 128], krh[one]], axis=1)
                score = lax.dot_general(left, right, (((1,), (1,)), ((), ())), preferred_element_type=F32)
                score = jnp.where(own, score[:, TOK:], score[:, :TOK]) + bias[...]
                top = jnp.max(score, axis=1, keepdims=True)
                weight = jnp.exp2((score - top) * SCALE)
                probs = weight * (1.0 / jnp.sum(weight, axis=1, keepdims=True))
                both = jnp.concatenate(
                    [jnp.where(own, 0.0, probs).astype(BF16), jnp.where(own, probs, 0.0).astype(BF16)], axis=1
                )
                got = jnp.dot(both, values[:, h * 128 : (h + 1) * 128], preferred_element_type=F32)
                ov[i, :, h * 128 : (h + 1) * 128] = got.astype(BF16)
        pltpu.make_async_copy(ov.at[i], out.at[:, pl.ds(i * 512, 512)], o_sem.at[i]).start()

    @pl.loop(0, FIRST)
    def _(i):
        attend(i)

    @pl.when(middle)
    def _():
        done(rs.at[pl.ds(0, 127)], recv1)
        rf[...] = rs[...].astype(F32).reshape(1024, 128)
        pages = jnp.concatenate([rf[pl.ds(t, 256, stride=4), :].astype(BF16) for t in range(4)], axis=1)
        picked = jnp.dot(onehot[...], pages, preferred_element_type=F32)
        for t in range(4):
            for k in range(4):
                of[pl.ds(t * 4 + k, 128, stride=16), :] = picked[k * 128 : (k + 1) * 128, t * 128 : (t + 1) * 128]
        os[...] = of[...].reshape(128, 16, 128).astype(BF16)
        for dg in range(8):
            for ds in range(16):
                if dg + ds:
                    a, b = (g + dg) % 8, (s + ds) % 16
                    remote(os.at[a * 16 + b], cb.at[my_chunk], send2, recv2, (a, b)).start()
        cb[my_chunk] = os[me]

    @pl.loop(FIRST, STEPS)
    def _(i):
        attend(i)

    @pl.when(middle)
    def _():
        done(cb.at[pl.ds(0, CHUNKS - 1)], recv2)

    @pl.when(jnp.logical_not(middle))
    def _():
        done(cb, recv2)

    cf[...] = cb[...].astype(F32).reshape(CHUNKS * 16, 128)
    half4 = lax.broadcasted_iota(jnp.int32, (4, 128), 1) < 64
    for quad in range(QUADS):
        for two in range(2):
            base = (quad * 2 + two) * 9

            def piece(tile, odd):
                return cf[pl.ds((quad * TILES + tile) * 16 + (2 * two + odd) * 4, 4), :]

            parts = (
                [piece(tile, 0) for tile in range(4)]
                + [jnp.where(half4, piece(4, 0), piece(0, 1))]
                + [piece(tile, 1) for tile in range(1, 5)]
            )
            for k, part in enumerate(parts):
                cout[:, (base + k) * 128 : (base + k + 1) * 128] = part.astype(BF16)
    last = pltpu.make_async_copy(cout, cache, c_sem)
    last.start()

    @pl.when(middle)
    def _():
        done(xs.at[pl.ds(0, CHUNKS - 1)], send1)
        done(os.at[pl.ds(0, 127)], send2)

    @pl.when(jnp.logical_not(middle))
    def _():
        done(xs, send1)

    @pl.when(has_right)
    def _():
        lat_copy.wait_send()
        rope_copy.wait_send()

    for i in range(STEPS):
        pltpu.make_async_copy(ov.at[i], out.at[:, pl.ds(i * 512, 512)], o_sem.at[i]).wait()
    last.wait()


def on_device(query, latent_raw, rope_raw, kv_gain, w_uk, w_uv, request_lengths, page_owner, page_slot):
    vmem = pl.BlockSpec(memory_space=pltpu.VMEM)
    anywhere = pl.BlockSpec(memory_space=pl.ANY)
    dma = pltpu.SemaphoreType.DMA
    return pl.pallas_call(
        kernel,
        out_shape=(
            jax.ShapeDtypeStruct((TOK, HEADS * 128), BF16),
            jax.ShapeDtypeStruct((4, PAGE_W), BF16),
        ),
        in_specs=[pl.BlockSpec(memory_space=pltpu.SMEM)] + [vmem] * 6 + [anywhere] * 3,
        out_specs=(anywhere, anywhere),
        scratch_shapes=[
            pltpu.VMEM((STEPS, TOK, 768), BF16),
            pltpu.VMEM((STEPS, LATENT, 512), BF16),
            pltpu.VMEM((STEPS, LATENT, 512), BF16),
            pltpu.VMEM((STEPS, TOK, 512), BF16),
            pltpu.VMEM((2 * TOK, LATENT), BF16),
            pltpu.VMEM((2 * TOK, TOK), BF16),
            pltpu.VMEM((2, 2 * TOK, TOK), BF16),
            pltpu.VMEM((TOK, TOK), F32),
            pltpu.VMEM((TOK, TOK), F32),
            pltpu.VMEM((TOK, TOK), F32),
            pltpu.VMEM((TILES, TOK, 128), F32),
            pltpu.VMEM((CHUNKS, 8, 128), BF16),
            pltpu.VMEM((128, 8, 128), BF16),
            pltpu.VMEM((1024, 128), F32),
            pltpu.VMEM((2048, 128), F32),
            pltpu.VMEM((128, 16, 128), BF16),
            pltpu.VMEM((CHUNKS, 16, 128), BF16),
            pltpu.VMEM((CHUNKS * 16, 128), F32),
            pltpu.VMEM((4, PAGE_W), BF16),
            pltpu.VMEM((512, 256), BF16),
            dma((STEPS,)),
            dma((STEPS,)),
            dma((STEPS,)),
            dma((STEPS,)),
            dma((2,)),
            dma((2,)),
            dma,
            dma,
            dma,
            dma,
            dma,
        ],
        compiler_params=pltpu.CompilerParams(
            collective_id=0, has_side_effects=True, vmem_limit_bytes=48 * 2**20
        ),
        name="prefill_and_pages",
    )(
        request_lengths,
        latent_raw,
        rope_raw,
        kv_gain.reshape(1, LATENT),
        page_owner.reshape(1, 256),
        page_slot.reshape(1, 256),
        jnp.asarray(trig_table()),
        query,
        w_uk,
        w_uv,
    )


def solution(mesh):
    rows = P(("group", "seq"), None)
    return jax.shard_map(
        on_device,
        mesh=mesh,
        in_specs=(rows, rows, rows, P(), P(), P(), P("group", None), P(), P()),
        out_specs=(rows, rows),
        check_vma=False,
    )
```

time: 478 us -> 54.4 us (0.11)
  the two profiles are of different devices: /device:TPU:74 before, /device:TPU:32 now
where the time goes in v1:
time: 54.4 us; the launch traced here: 54 us
  Pallas kernels  44.1 us (81%)
  local copies, waits for them, and re-layouts  9.27 us (17%)
  between operations  0.65 us (1%)
    pallas_call x1, Pallas kernels, on_device(): pl.pallas_call(kernel, out_shape=(jax.ShapeDtypeStruct((TOK, HEADS * 128)...  44.1 us
    unnamed x17, local copies, waits for them, and re-layouts  9.27 us

profile of v1, /device:TPU:32, one launch (start us, length us, event | category | flops | bytes accessed | tf_op | source)
XLA Modules:
  0.0 54.0 jit_solution(7454719886618494151)
XLA Ops:
  0.6 0.8 %copy.12.rope_raw = bf16[128,64]{1,0:T(8,128)(2,1)S(1)} copy(bf16[128,64]{0,1:T(8,128)(2,1)} %param.12) | data formatting | bytes 32768 | tf_op args[2]
  1.5 0.0 copy-start
  1.5 1.9 %copy-done = bf16[128,12288]{1,0:T(8,128)(2,1)S(1)} copy-done((bf16[128,12288]{1,0:T(8,128)(2,1)S(1)}, bf16[128,12288]{1,0:T(8,128)(2,1)}, u32[]{:S(2)}) %copy-start) | copy-done | bytes 3145752
  3.4 0.0 copy-start.1
  3.4 0.9 %copy-done.1 = bf16[384,256]{1,0:T(8,128)(2,1)S(1)} copy-done((bf16[384,256]{1,0:T(8,128)(2,1)S(1)}, bf16[384,256]{1,0:T(8,128)(2,1)}, u32[]{:S(2)}) %copy-start.1) | copy-done | bytes 196632
  4.3 0.0 copy-start.2
  4.3 0.9 %copy-done.2 = bf16[128,512]{1,0:T(8,128)(2,1)S(1)} copy-done((bf16[128,512]{1,0:T(8,128)(2,1)S(1)}, bf16[128,512]{1,0:T(8,128)(2,1)}, u32[]{:S(2)}) %copy-start.2) | copy-done | bytes 131096
  5.2 0.0 copy-start.3
  5.2 0.7 %copy-done.3 = f32[512]{0:T(512)S(1)} copy-done((f32[512]{0:T(512)S(1)}, f32[512]{0:T(512)}, u32[]{:S(2)}) %copy-start.3) | copy-done | bytes 2072
  5.9 0.0 copy-start.4
  5.9 0.7 %copy-done.4 = s32[256]{0:T(256)S(1)} copy-done((s32[256]{0:T(256)S(1)}, s32[256]{0:T(256)}, u32[]{:S(2)}) %copy-start.4) | copy-done | bytes 1048
  6.6 0.0 copy-start.5
  6.6 0.7 %copy-done.5 = s32[256]{0:T(256)S(1)} copy-done((s32[256]{0:T(256)S(1)}, s32[256]{0:T(256)}, u32[]{:S(2)}) %copy-start.5) | copy-done | bytes 1048
  7.2 0.0 copy-start.6
  7.2 0.7 %copy-done.6 = s32[1,32]{1,0:T(1,128)S(1)} copy-done((s32[1,32]{1,0:T(1,128)S(1)}, s32[1,32]{1,0:T(1,128)}, u32[]{:S(2)}) %copy-start.6) | copy-done | bytes 152
  7.9 44.1 %prefill_and_pages.1 = (bf16[128,8192]{1,0:T(8,128)(2,1)S(1)}, bf16[4,36864]{1,0:T(4,128)(2,1)S(1)}) custom-call(s32[1,32]{1,0:T(1,128)S(1)} %copy-done.6, bf16[128,512]{1,0:T(8,128)(2,1)S(1)} %copy-done.2, bf16[128,64]{1,0:T(8,128)(2,1)S(1)} %copy.12.rope_raw, f32[1,512]{1,0:T(1,128)S(1)} %bitcast.3, s32[1,256]{1,0:T(1,128)S(1)} %bitcast.4, ...), custom_call_target="tpu_custom_call" | custom-call | tf_op jit(solution)/shard_map/prefill_and_pages/pallas_call | solution.py:301
  52.0 1.3 %copy.15 = bf16[128,8192]{1,0:T(8,128)(2,1)} copy(bf16[128,8192]{1,0:T(8,128)(2,1)S(1)} %get-tuple-element.4) | data formatting | bytes 4194304
  53.3 0.7 %copy.16 = bf16[4,36864]{1,0:T(4,128)(2,1)} copy(bf16[4,36864]{1,0:T(4,128)(2,1)S(1)} %get-tuple-element.5) | data formatting | bytes 589824
Async XLA Ops:
  1.5 1.9 %copy-start = (bf16[128,12288]{1,0:T(8,128)(2,1)S(1)}, bf16[128,12288]{1,0:T(8,128)(2,1)}, u32[]{:S(2)}) copy-start(bf16[128,12288]{1,0:T(8,128)(2,1)} %query.1) | copy-start | bytes 9437188
  3.4 0.9 %copy-start.1 = (bf16[384,256]{1,0:T(8,128)(2,1)S(1)}, bf16[384,256]{1,0:T(8,128)(2,1)}, u32[]{:S(2)}) copy-start(bf16[384,256]{1,0:T(8,128)(2,1)} %constant.2.clone.trig) | copy-start | bytes 589828
  4.3 0.9 %copy-start.2 = (bf16[128,512]{1,0:T(8,128)(2,1)S(1)}, bf16[128,512]{1,0:T(8,128)(2,1)}, u32[]{:S(2)}) copy-start(bf16[128,512]{1,0:T(8,128)(2,1)} %latent_raw.1) | copy-start | bytes 393220
  5.2 0.7 %copy-start.3 = (f32[512]{0:T(512)S(1)}, f32[512]{0:T(512)}, u32[]{:S(2)}) copy-start(f32[512]{0:T(512)} %param.13) | copy-start | bytes 6148
  5.9 0.7 %copy-start.4 = (s32[256]{0:T(256)S(1)}, s32[256]{0:T(256)}, u32[]{:S(2)}) copy-start(s32[256]{0:T(256)} %param.17) | copy-start | bytes 3076
  6.6 0.7 %copy-start.5 = (s32[256]{0:T(256)S(1)}, s32[256]{0:T(256)}, u32[]{:S(2)}) copy-start(s32[256]{0:T(256)} %param.18) | copy-start | bytes 3076
  7.2 0.7 %copy-start.6 = (s32[1,32]{1,0:T(1,128)S(1)}, s32[1,32]{1,0:T(1,128)}, u32[]{:S(2)}) copy-start(s32[1,32]{1,0:T(1,128)} %lengths.1) | copy-start | bytes 388

commit v2 on v1

--- a/solution.py
+++ b/solution.py
@@ -18,8 +18,11 @@
 QUADS = 16
 TILES = 5
 CHUNKS = QUADS * TILES
-STEPS = 16
-FIRST = 11
+STEPS = 8
+WIDE = 1024
+QWIDE = 1536
+HEADS_STEP = 8
+SPLIT = 2
 PAGE_W = 36864
 SCALE = float(1.0 / 192.0**0.5 * np.log2(np.e))
 
@@ -60,11 +63,14 @@
 
 
 def kernel(
-    lengths, latent_raw, rope_raw, gain, owner, slot, trig, query, w_uk, w_uv,
+    lengths, gain, latent_raw, rope_raw, trig, owner, slot, query, w_uk, w_uv,
     out, cache,
-    qv, kv, vv, ov, lat2, kr2, krh, cos_v, sin_v, bias, ypage, xs, rs, rf, of, os, cb, cf, cout, onehot,
-    q_sem, k_sem, v_sem, o_sem, send_n, recv_n, send1, recv1, send2, recv2, c_sem,
+    lengths_s, gain_v, latent_v, rope_v, trig_v, owner_v, slot_v,
+    qv, kv, vv, ov, lat2, kr2, cos_v, sin_v, bias, low_m, up_m, ypage, xs, rs, rf, of, os, cb, cf, cout, onehot,
+    left0, left1, right0, right1, value0, value1, score_v, prob_v,
+    in_sem, q_sem, k_sem, v_sem, o_sem, send_n, recv_n, send1, recv1, send2, recv2, c_sem,
 ):
+    lefts, rights, valued = (left0, left1), (right0, right1), (value0, value1)
     g, s = lax.axis_index("group"), lax.axis_index("seq")
     me = g * 16 + s
     core, y = g % 2, g // 2
@@ -73,6 +79,34 @@
     my_tile = jnp.where(core == 0, y, 4)
     my_chunk = s * TILES + my_tile
     has_left, has_right = s > 0, s < 15
+
+    small = [
+        pltpu.make_async_copy(src, dst, in_sem.at[i])
+        for i, (src, dst) in enumerate(
+            (
+                (latent_raw, latent_v),
+                (lengths, lengths_s),
+                (rope_raw, rope_v),
+                (trig, trig_v),
+                (gain, gain_v),
+                (owner, owner_v),
+                (slot, slot_v),
+            )
+        )
+    ]
+    for copy in small:
+        copy.start()
+
+    def fetches(i):
+        return (
+            pltpu.make_async_copy(query.at[:, pl.ds(i * QWIDE, QWIDE)], qv.at[i], q_sem.at[i]),
+            pltpu.make_async_copy(w_uk.at[:, pl.ds(i * WIDE, WIDE)], kv.at[i], k_sem.at[i]),
+            pltpu.make_async_copy(w_uv.at[:, pl.ds(i * WIDE, WIDE)], vv.at[i], v_sem.at[i]),
+        )
+
+    def fetched(i):
+        for fetch in fetches(i):
+            fetch.wait()
 
     barrier = pltpu.get_barrier_semaphore()
 
@@ -102,13 +136,6 @@
     def _():
         greet((g, s - 1))
 
-    def fetches(i):
-        return (
-            pltpu.make_async_copy(query.at[:, pl.ds(i * 768, 768)], qv.at[i], q_sem.at[i]),
-            pltpu.make_async_copy(w_uk.at[:, pl.ds(i * 512, 512)], kv.at[i], k_sem.at[i]),
-            pltpu.make_async_copy(w_uv.at[:, pl.ds(i * 512, 512)], vv.at[i], v_sem.at[i]),
-        )
-
     for i in range(STEPS):
         for fetch in fetches(i):
             fetch.start()
@@ -118,25 +145,29 @@
     low = col % 64 < 32
     half = col < 64
     index = row + s * TOK
+    for copy in small[:2]:
+        copy.wait()
     begin = jnp.zeros((TOK, TOK), jnp.int32)
     start = jnp.int32(0)
     for r in range(32):
         begin = jnp.where(index >= start, start, begin)
-        start = start + lengths[0, r]
+        start = start + lengths_s[0, r]
     pos = index - begin
     hot = (col == pos).astype(F32).astype(BF16)
-    angles = jnp.dot(jnp.concatenate([hot, hot, hot], axis=1), trig[...], preferred_element_type=F32)
+    for copy in small[2:]:
+        copy.wait()
+    angles = jnp.dot(jnp.concatenate([hot, hot, hot], axis=1), trig_v[...], preferred_element_type=F32)
     cosine, sine = angles[:, :TOK], angles[:, TOK:]
     cos_v[...] = cosine
     sin_v[...] = sine
-    bias[...] = jnp.where((row - col + TOK) % TOK <= pos, 0.0, -1e30)
-
-    source = latent_raw[...].astype(F32)
+
+    source = latent_v[...].astype(F32)
     norm = lax.rsqrt(jnp.mean(source * source, axis=1, keepdims=True) + 1e-06)
-    latent = (source * norm * gain[...]).astype(BF16)
+    latent = (source * norm * gain_v[...]).astype(BF16)
     lat2[TOK:, :] = latent
-    rope = rope_raw[...].astype(F32)
-    key_rope = rotated(jnp.concatenate([rope, rope], axis=1), cosine, sine, low).astype(BF16)
+    rope = rope_v[...].astype(F32)
+    rope = jnp.concatenate([rope, rope], axis=0).T
+    key_rope = rotated(rope, cosine, sine, low).astype(BF16)
     kr2[TOK:, :] = key_rope
 
     wide, tail = latent.astype(F32), key_rope.astype(F32)
@@ -172,10 +203,16 @@
         lambda quad, tile, device: remote(xs.at[quad * TILES + tile], rs.at[me], send1, recv1, device).start()
     )
 
+    bias[...] = jnp.where((row - col + TOK) % TOK <= pos, 0.0, -1e30)
+    low_m[...] = jnp.where(col <= row, 1.0, 0.0).astype(BF16)
+    up_m[...] = jnp.where(col <= row, 0.0, 1.0).astype(BF16)
+    for value in valued:
+        value[:, :, TOK:] = jnp.ones((HEADS_STEP, 2 * TOK, TOK), BF16)
+
     @pl.when(middle)
     def _():
         rs[me] = xs[my_chunk]
-        want = slot[...] * 128 + owner[...]
+        want = slot_v[...] * 128 + owner_v[...]
         onehot[...] = (lax.broadcasted_iota(jnp.int32, (512, 256), 0) == want).astype(F32).astype(BF16)
 
     @pl.when(has_left)
@@ -188,44 +225,75 @@
         lat2[:TOK, :] = jnp.zeros((TOK, LATENT), BF16)
         kr2[:TOK, :] = jnp.zeros((TOK, TOK), BF16)
 
-    half2 = lax.broadcasted_iota(jnp.int32, (2 * TOK, TOK), 1) < 64
-    ropes = kr2[...].astype(F32)
-    krh[0] = jnp.where(half2, ropes, 0.0).astype(BF16)
-    krh[1] = jnp.where(half2, 0.0, ropes).astype(BF16)
-
-    def attend(i):
-        for fetch in fetches(i):
-            fetch.wait()
-        keys = jnp.dot(lat2[...], kv[i], preferred_element_type=F32).astype(BF16)
-        values = jnp.dot(lat2[...], vv[i], preferred_element_type=F32).astype(BF16)
+    ropes = kr2[...].astype(F32).T
+    first_half = lax.broadcasted_iota(jnp.int32, (TOK, 2 * TOK), 0) < 64
+    for one in range(2):
+        masked = jnp.where(first_half if one == 0 else ~first_half, ropes, 0.0).astype(BF16)
+        for right in rights:
+            for pair in range(HEADS_STEP // 2):
+                right[2 * pair + one, TOK:, :] = masked
+
+    def prepare(i, b):
+        col = lax.broadcasted_iota(jnp.int32, (TOK, TOK), 1)
+        half = col < 64
+        low = col % 64 < 32
+        for pair in range(HEADS_STEP // 2):
+            columns = slice(pair * 256, pair * 256 + 256)
+            keys = jnp.dot(lat2[...], kv[i, :, columns], preferred_element_type=F32).astype(BF16)
+            values = jnp.dot(lat2[...], vv[i, :, columns], preferred_element_type=F32).astype(BF16)
+            for one in range(2):
+                rights[b][2 * pair + one, :TOK, :] = keys[:, one * 128 : one * 128 + 128].T
+                valued[b][2 * pair + one, :, :TOK] = values[:, one * 128 : one * 128 + 128]
+            t0, t1, t2 = [qv[i, :, pl.ds(pair * 384 + t * 128, 128)] for t in range(3)]
+            ropes = jnp.where(half, t1, t2).astype(F32)
+            turn = rotated(ropes, cos_v[...], sin_v[...], low).astype(BF16)
+            second = pltpu.roll(jnp.where(half, t2, t1).astype(F32), 64, 1).astype(BF16)
+            for one, nope in enumerate((t0, second)):
+                lefts[b][2 * pair + one, :, :TOK] = nope
+                lefts[b][2 * pair + one, :, TOK:] = turn
+
+    def scored(b, h):
         row = lax.broadcasted_iota(jnp.int32, (TOK, TOK), 0)
         col = lax.broadcasted_iota(jnp.int32, (TOK, TOK), 1)
-        own = col <= row
-        half = col < 64
-        low = col % 64 < 32
-        for pair in range(2):
-            tiles = [qv[i, :, pl.ds(pair * 384 + t * 128, 128)].astype(F32) for t in range(3)]
-            turn = rotated(jnp.where(half, tiles[1], tiles[2]), cos_v[...], sin_v[...], low).astype(BF16)
-            second = pltpu.roll(jnp.where(half, tiles[2], tiles[1]), 64, 1).astype(BF16)
-            for one, nope in enumerate((tiles[0].astype(BF16), second)):
-                h = 2 * pair + one
-                left = jnp.concatenate([nope, turn], axis=1)
-                right = jnp.concatenate([keys[:, h * 128 : (h + 1) * 128], krh[one]], axis=1)
-                score = lax.dot_general(left, right, (((1,), (1,)), ((), ())), preferred_element_type=F32)
-                score = jnp.where(own, score[:, TOK:], score[:, :TOK]) + bias[...]
-                top = jnp.max(score, axis=1, keepdims=True)
-                weight = jnp.exp2((score - top) * SCALE)
-                probs = weight * (1.0 / jnp.sum(weight, axis=1, keepdims=True))
-                both = jnp.concatenate(
-                    [jnp.where(own, 0.0, probs).astype(BF16), jnp.where(own, probs, 0.0).astype(BF16)], axis=1
-                )
-                got = jnp.dot(both, values[:, h * 128 : (h + 1) * 128], preferred_element_type=F32)
-                ov[i, :, h * 128 : (h + 1) * 128] = got.astype(BF16)
-        pltpu.make_async_copy(ov.at[i], out.at[:, pl.ds(i * 512, 512)], o_sem.at[i]).start()
-
-    @pl.loop(0, FIRST)
-    def _(i):
-        attend(i)
+        score = jnp.dot(lefts[b][h], rights[b][h], preferred_element_type=F32)
+        score_v[h] = jnp.where(col <= row, score[:, TOK:], score[:, :TOK]) + bias[...]
+
+    def softened(h):
+        score = score_v[h]
+        top = jnp.max(score, axis=1, keepdims=True)
+        weight = jnp.exp2((score - top) * SCALE).astype(BF16)
+        prob_v[h, :, :TOK] = weight * up_m[...]
+        prob_v[h, :, TOK:] = weight * low_m[...]
+
+    def summed(i, b, h):
+        got = jnp.dot(prob_v[h], valued[b][h], preferred_element_type=F32)
+        ov[i, :, h * 128 : (h + 1) * 128] = (got[:, :TOK] * (1.0 / got[:, TOK:])).astype(BF16)
+
+    def result(i):
+        return pltpu.make_async_copy(ov.at[i], out.at[:, pl.ds(i * WIDE, WIDE)], o_sem.at[i])
+
+    def step(i, b):
+        if b == 0:
+            fetched(i + 1)
+        else:
+            pl.when(i + 1 < STEPS)(lambda: fetched(i + 1))
+        for h in range(HEADS_STEP + 4):
+            if h < HEADS_STEP:
+                scored(b, h)
+            if 0 <= h - 2 < HEADS_STEP:
+                softened(h - 2)
+            if 0 <= h - 4 < HEADS_STEP:
+                summed(i, b, h - 4)
+        prepare(jnp.minimum(i + 1, STEPS - 1), 1 - b)
+        result(i).start()
+
+    fetched(0)
+    prepare(0, 0)
+
+    @pl.loop(0, SPLIT)
+    def _(j):
+        for b in range(2):
+            step(2 * j + b, b)
 
     @pl.when(middle)
     def _():
@@ -237,16 +305,27 @@
             for k in range(4):
                 of[pl.ds(t * 4 + k, 128, stride=16), :] = picked[k * 128 : (k + 1) * 128, t * 128 : (t + 1) * 128]
         os[...] = of[...].reshape(128, 16, 128).astype(BF16)
-        for dg in range(8):
-            for ds in range(16):
-                if dg + ds:
-                    a, b = (g + dg) % 8, (s + ds) % 16
-                    remote(os.at[a * 16 + b], cb.at[my_chunk], send2, recv2, (a, b)).start()
         cb[my_chunk] = os[me]
 
-    @pl.loop(FIRST, STEPS)
-    def _(i):
-        attend(i)
+    groups = 8 // (2 * (STEPS // 2 - SPLIT))
+
+    @pl.loop(SPLIT, STEPS // 2)
+    def _(j):
+        for b in range(2):
+
+            @pl.when(middle)
+            def _():
+                for k in range(groups):
+                    dg = ((j - SPLIT) * 2 + b) * groups + k
+                    for ds in range(16):
+                        a, c = (g + dg) % 8, (s + ds) % 16
+                        send = remote(os.at[a * 16 + c], cb.at[my_chunk], send2, recv2, (a, c))
+                        if ds:
+                            send.start()
+                        else:
+                            pl.when(dg > 0)(send.start)
+
+            step(2 * j + b, b)
 
     @pl.when(middle)
     def _():
@@ -290,43 +369,66 @@
         rope_copy.wait_send()
 
     for i in range(STEPS):
-        pltpu.make_async_copy(ov.at[i], out.at[:, pl.ds(i * 512, 512)], o_sem.at[i]).wait()
+        result(i).wait()
     last.wait()
 
 
 def on_device(query, latent_raw, rope_raw, kv_gain, w_uk, w_uv, request_lengths, page_owner, page_slot):
-    vmem = pl.BlockSpec(memory_space=pltpu.VMEM)
-    anywhere = pl.BlockSpec(memory_space=pl.ANY)
+    hbm = pl.BlockSpec(memory_space=pltpu.HBM)
     dma = pltpu.SemaphoreType.DMA
+
+    def b16(*shape):
+        return pltpu.VMEM(shape, BF16)
+
+    def f32(*shape):
+        return pltpu.VMEM(shape, F32)
+
     return pl.pallas_call(
         kernel,
         out_shape=(
             jax.ShapeDtypeStruct((TOK, HEADS * 128), BF16),
             jax.ShapeDtypeStruct((4, PAGE_W), BF16),
         ),
-        in_specs=[pl.BlockSpec(memory_space=pltpu.SMEM)] + [vmem] * 6 + [anywhere] * 3,
-        out_specs=(anywhere, anywhere),
+        in_specs=[hbm] * 10,
+        out_specs=(hbm, hbm),
         scratch_shapes=[
-            pltpu.VMEM((STEPS, TOK, 768), BF16),
-            pltpu.VMEM((STEPS, LATENT, 512), BF16),
-            pltpu.VMEM((STEPS, LATENT, 512), BF16),
-            pltpu.VMEM((STEPS, TOK, 512), BF16),
-            pltpu.VMEM((2 * TOK, LATENT), BF16),
-            pltpu.VMEM((2 * TOK, TOK), BF16),
-            pltpu.VMEM((2, 2 * TOK, TOK), BF16),
-            pltpu.VMEM((TOK, TOK), F32),
-            pltpu.VMEM((TOK, TOK), F32),
-            pltpu.VMEM((TOK, TOK), F32),
-            pltpu.VMEM((TILES, TOK, 128), F32),
-            pltpu.VMEM((CHUNKS, 8, 128), BF16),
-            pltpu.VMEM((128, 8, 128), BF16),
-            pltpu.VMEM((1024, 128), F32),
-            pltpu.VMEM((2048, 128), F32),
-            pltpu.VMEM((128, 16, 128), BF16),
-            pltpu.VMEM((CHUNKS, 16, 128), BF16),
-            pltpu.VMEM((CHUNKS * 16, 128), F32),
-            pltpu.VMEM((4, PAGE_W), BF16),
-            pltpu.VMEM((512, 256), BF16),
+            pltpu.SMEM((1, 32), jnp.int32),
+            f32(1, LATENT),
+            b16(TOK, LATENT),
+            b16(64, TOK),
+            b16(384, 256),
+            pltpu.VMEM((1, 256), jnp.int32),
+            pltpu.VMEM((1, 256), jnp.int32),
+            b16(STEPS, TOK, QWIDE),
+            b16(STEPS, LATENT, WIDE),
+            b16(STEPS, LATENT, WIDE),
+            b16(STEPS, TOK, WIDE),
+            b16(2 * TOK, LATENT),
+            b16(2 * TOK, TOK),
+            f32(TOK, TOK),
+            f32(TOK, TOK),
+            f32(TOK, TOK),
+            b16(TOK, TOK),
+            b16(TOK, TOK),
+            f32(TILES, TOK, 128),
+            b16(CHUNKS, 8, 128),
+            b16(128, 8, 128),
+            f32(1024, 128),
+            f32(2048, 128),
+            b16(128, 16, 128),
+            b16(CHUNKS, 16, 128),
+            f32(CHUNKS * 16, 128),
+            b16(4, PAGE_W),
+            b16(512, 256),
+            b16(HEADS_STEP, TOK, 256),
+            b16(HEADS_STEP, TOK, 256),
+            b16(HEADS_STEP, 256, 256),
+            b16(HEADS_STEP, 256, 256),
+            b16(HEADS_STEP, 256, 256),
+            b16(HEADS_STEP, 256, 256),
+            f32(HEADS_STEP, TOK, TOK),
+            b16(HEADS_STEP, TOK, 256),
+            dma((7,)),
             dma((STEPS,)),
             dma((STEPS,)),
             dma((STEPS,)),
@@ -340,17 +442,17 @@
             dma,
         ],
         compiler_params=pltpu.CompilerParams(
-            collective_id=0, has_side_effects=True, vmem_limit_bytes=48 * 2**20
+            collective_id=0, has_side_effects=True, vmem_limit_bytes=56 * 2**20
         ),
         name="prefill_and_pages",
     )(
         request_lengths,
+        kv_gain.reshape(1, LATENT),
         latent_raw,
-        rope_raw,
-        kv_gain.reshape(1, LATENT),
+        rope_raw.T,
+        jnp.asarray(trig_table()),
         page_owner.reshape(1, 256),
         page_slot.reshape(1, 256),
-        jnp.asarray(trig_table()),
         query,
         w_uk,
         w_uv,

time: 54.4 us -> 39.3 us (0.72)
  the two profiles are of different devices: /device:TPU:32 before, /device:TPU:1 now
where the time goes in v2:
time: 39.3 us; the launch traced here: 39.1 us
  Pallas kernels  34.6 us (88%)
  local copies, waits for them, and re-layouts  3.86 us (10%)
  between operations  0.65 us (2%)
    pallas_call x1, Pallas kernels, on_device(): pl.pallas_call(kernel, out_shape=(jax.ShapeDtypeStruct((TOK, HEADS * 128)...  34.6 us
    unnamed x4, local copies, waits for them, and re-layouts  3.86 us

profile of v2, /device:TPU:1, one launch (start us, length us, event | category | flops | bytes accessed | tf_op | source)
XLA Modules:
  0.0 39.1 jit_solution(16366406870258652561)
XLA Ops:
  0.6 34.6 %prefill_and_pages.1 = (bf16[128,8192]{1,0:T(8,128)(2,1)}, bf16[4,36864]{1,0:T(4,128)(2,1)}) custom-call(s32[1,32]{1,0:T(1,128)} %lengths.1, f32[1,512]{1,0:T(1,128)} %bitcast.5, bf16[128,512]{1,0:T(8,128)(2,1)} %latent_raw.1, bf16[64,128]{1,0:T(8,128)(2,1)} %bitcast.4, bf16[384,256]{1,0:T(8,128)(2,1)} %constant.2.clone.trig, s32[1,256]{1,0:T(1,128)} %bitcast.6, ...), custom_call_target="tpu_custom_call" | custom-call | tf_op jit(solution)/shard_map/prefill_and_pages/pallas_call | solution.py:386
  35.3 0.0 copy-start
  35.3 3.1 %copy.14 = bf16[128,8192]{1,0:T(8,128)(2,1)} copy(bf16[128,8192]{1,0:T(8,128)(2,1)} %get-tuple-element.4) | data formatting | bytes 4194304
  38.4 0.0 copy-done
  38.4 0.7 %copy.15 = bf16[4,36864]{1,0:T(4,128)(2,1)} copy(bf16[4,36864]{1,0:T(4,128)(2,1)S(1)} %copy-done) | data formatting | bytes 589824
Async XLA Ops:
  35.3 3.2 %copy-start = (bf16[4,36864]{1,0:T(4,128)(2,1)S(1)}, bf16[4,36864]{1,0:T(4,128)(2,1)}, u32[]{:S(2)}) copy-start(bf16[4,36864]{1,0:T(4,128)(2,1)} %get-tuple-element.5) | copy-start | bytes 884740

commit v3 on v2

v3 whole, which is shorter than its diff:
```python
import functools

import jax
import jax.numpy as jnp
import numpy as np
from jax import lax
from jax.experimental import pallas as pl
from jax.experimental.pallas import tpu as pltpu
from jax.sharding import PartitionSpec as P
import ml_dtypes

MESH = pl.DeviceIdType.MESH
F32 = jnp.float32
BF16 = jnp.bfloat16
TOK = 128
HEADS = 64
LATENT = 512
QUADS = 16
TILES = 5
CHUNKS = QUADS * TILES
STEPS = 8
WIDE = 1024
QWIDE = 1536
HEADS_STEP = 8
MIDS = 10
PAGE_W = 36864
SCALE = float(1.0 / 192.0**0.5 * np.log2(np.e))


def trig_table():
    freqs = (10000.0 ** (-np.arange(32, dtype=np.float64) / 32.0)).astype(np.float32)
    angle = np.arange(TOK, dtype=np.float32)[:, None] * freqs[None, :]
    cosine = np.cos(angle.astype(np.float64)).astype(np.float32)
    sine = np.sin(angle.astype(np.float64)).astype(np.float32)
    full = np.concatenate([cosine] * 4 + [-sine, sine, -sine, sine], axis=1)
    parts = []
    for _ in range(3):
        part = full.astype(ml_dtypes.bfloat16)
        parts.append(part)
        full = full - part.astype(np.float32)
    return np.concatenate(parts, axis=0)


def remote(src, dst, send, recv, device):
    return pltpu.make_async_remote_copy(
        src_ref=src, dst_ref=dst, send_sem=send, recv_sem=recv, device_id=device, device_id_type=MESH
    )


def done(ref, sem):
    pltpu.make_async_copy(ref, ref, sem).wait()


def rotated(x, cosine, sine, low):
    partner = jnp.where(low, pltpu.roll(x, 96, 1), pltpu.roll(x, 32, 1))
    return x * cosine + partner * sine


def kernel(
    lengths, gain, latent_raw, rope_raw, trig, owner, slot, query, w_uk, w_uv,
    out, cache,
    lengths_s, gain_v, latent_v, rope_v, trig_v, owner_v, slot_v,
    qv, kv, vv, lat2, kr2, cos_v, sin_v, bias, low_m, up_m, ypage, xs, rs, rf, of, os, cb, cf, onehot,
    left0, left1, right0, right1, value0, value1, score_v, prob_v,
    in_sem, q_sem, k_sem, v_sem, send_n, recv_n, send1, recv1, send2, recv2,
):
    lefts, rights, valued = (left0, left1), (right0, right1), (value0, value1)
    g, s = lax.axis_index("group"), lax.axis_index("seq")
    me = g * 16 + s
    middle = s < MIDS
    my_chunk = jnp.where(middle, s * 8 + g, 0)
    has_left, has_right = s > 0, s < 15
    early = s < 8

    small = [
        pltpu.make_async_copy(src, dst, in_sem.at[i])
        for i, (src, dst) in enumerate(
            (
                (latent_raw, latent_v),
                (gain, gain_v),
                (lengths, lengths_s),
                (rope_raw, rope_v),
                (trig, trig_v),
                (owner, owner_v),
                (slot, slot_v),
            )
        )
    ]
    for copy in small:
        copy.start()

    def fetches(i):
        return (
            pltpu.make_async_copy(query.at[:, pl.ds(i * QWIDE, QWIDE)], qv.at[i], q_sem.at[i]),
            pltpu.make_async_copy(w_uk.at[:, pl.ds(i * WIDE, WIDE)], kv.at[i], k_sem.at[i]),
            pltpu.make_async_copy(w_uv.at[:, pl.ds(i * WIDE, WIDE)], vv.at[i], v_sem.at[i]),
        )

    def fetched(i):
        for fetch in fetches(i):
            fetch.wait()

    barrier = pltpu.get_barrier_semaphore()

    def greet(device):
        pl.semaphore_signal(barrier, inc=1, device_id=device, device_id_type=MESH)

    @pl.when(middle)
    def _():
        for b in range(16):
            for a in range(8):
                pl.when(me != a * 16 + b)(functools.partial(greet, (a, b)))

    @pl.when(has_left)
    def _():
        greet((g, s - 1))

    for i in range(STEPS):
        for fetch in fetches(i):
            fetch.start()

    row = lax.broadcasted_iota(jnp.int32, (TOK, TOK), 0)
    col = lax.broadcasted_iota(jnp.int32, (TOK, TOK), 1)
    low = col % 64 < 32
    half = col < 64
    odd = row % 2 == 1
    upper = lax.broadcasted_iota(jnp.int32, (8, 128), 0) < 4

    for copy in small[:2]:
        copy.wait()
    source = latent_v[...].astype(F32)
    norm = lax.rsqrt(jnp.mean(source * source, axis=1, keepdims=True) + 1e-06)
    latent = (source * norm * gain_v[...]).astype(BF16)
    lat2[TOK:, :] = latent

    wide = latent.astype(F32)
    plain = [wide[:, i * 128 : (i + 1) * 128] for i in range(4)]
    turned = [pltpu.roll(x, 64, 1) for x in plain]
    moved = [turned[0]] + [jnp.where(half, turned[i - 1], turned[i]) for i in range(1, 4)]

    def chunked(tile):
        for octet in range(8):
            first = ypage[tile, octet * 8 : octet * 8 + 8, :]
            second = ypage[tile, 64 + octet * 8 : 64 + octet * 8 + 8, :]
            xs[tile * QUADS + 2 * octet] = jnp.where(upper, first, pltpu.roll(second, 4, 0)).astype(BF16)
            xs[tile * QUADS + 2 * octet + 1] = jnp.where(upper, pltpu.roll(first, 4, 0), second).astype(BF16)

    for tile, (a, b) in enumerate(zip(plain, moved)):
        ypage[tile] = jnp.where(odd, b, a)
    for tile in range(4):
        chunked(tile)

    pl.semaphore_wait(barrier, 8 * MIDS - jnp.where(middle, 1, 0) + jnp.where(has_right, 1, 0))

    lat_copy = remote(lat2.at[pl.ds(TOK, TOK)], lat2.at[pl.ds(0, TOK)], send_n.at[0], recv_n.at[0], (g, s + 1))
    rope_copy = remote(kr2.at[pl.ds(TOK, TOK)], kr2.at[pl.ds(0, TOK)], send_n.at[1], recv_n.at[1], (g, s + 1))
    pl.when(has_right & early)(lat_copy.start)

    def first_hop(b):
        for a in range(8):
            copy = remote(xs.at[b * 8 + a], rs.at[me], send1, recv1, (a, b))
            pl.when(me != a * 16 + b)(copy.start)

    for b in range(8):
        first_hop(b)

    for copy in small[2:]:
        copy.wait()
    index = lax.broadcasted_iota(jnp.int32, (8, TOK), 1) + s * TOK
    begin = jnp.zeros((8, TOK), jnp.int32)
    start = jnp.int32(0)
    for r in range(32):
        begin = jnp.where(index >= start, start, begin)
        start = start + lengths_s[0, r]
    pos = (index - begin).astype(F32)
    pos = jnp.concatenate([pos] * 16, axis=0).T.astype(jnp.int32)
    hot = (col == pos).astype(F32).astype(BF16)
    angles = jnp.dot(jnp.concatenate([hot, hot, hot], axis=1), trig_v[...], preferred_element_type=F32)
    cosine, sine = angles[:, :TOK], angles[:, TOK:]
    rope = rope_v[...].astype(F32)
    rope = jnp.concatenate([rope, rope], axis=0).T
    key_rope = rotated(rope, cosine, sine, low).astype(BF16)
    kr2[TOK:, :] = key_rope
    tail = key_rope.astype(F32)
    last_lanes = pltpu.roll(lat2[TOK:, 384:].astype(F32), 64, 1)
    ypage[4] = jnp.where(odd, jnp.where(half, last_lanes, tail), tail)
    chunked(4)
    pl.when(has_right)(rope_copy.start)
    for b in range(8, MIDS):
        first_hop(b)
    pl.when(has_right & jnp.logical_not(early))(lat_copy.start)

    cos_v[...] = cosine
    sin_v[...] = sine
    bias[...] = jnp.where((row - col + TOK) % TOK <= pos, 0.0, -1e30)
    low_m[...] = jnp.where(col <= row, 1.0, 0.0).astype(BF16)
    up_m[...] = jnp.where(col <= row, 0.0, 1.0).astype(BF16)
    for value in valued:
        value[:, :, TOK:] = jnp.ones((HEADS_STEP, 2 * TOK, TOK), BF16)

    @pl.when(middle)
    def _():
        rs[me] = xs[my_chunk]
        want = slot_v[...] * 128 + owner_v[...]
        onehot[...] = (lax.broadcasted_iota(jnp.int32, (512, 256), 0) == want).astype(F32).astype(BF16)

    @pl.when(has_left)
    def _():
        done(lat2.at[pl.ds(0, TOK)], recv_n.at[0])
        done(kr2.at[pl.ds(0, TOK)], recv_n.at[1])

    @pl.when(s == 0)
    def _():
        lat2[:TOK, :] = jnp.zeros((TOK, LATENT), BF16)
        kr2[:TOK, :] = jnp.zeros((TOK, TOK), BF16)

    ropes = kr2[...].astype(F32).T
    first_half = lax.broadcasted_iota(jnp.int32, (TOK, 2 * TOK), 0) < 64
    for one in range(2):
        masked = jnp.where(first_half if one == 0 else ~first_half, ropes, 0.0).astype(BF16)
        for right in rights:
            for pair in range(HEADS_STEP // 2):
                right[2 * pair + one, TOK:, :] = masked

    def prepare(i, b, piece):
        pair = piece // 2
        columns = slice(pair * 256, pair * 256 + 256)
        if piece % 2:
            values = jnp.dot(lat2[...], vv[i, :, columns], preferred_element_type=F32).astype(BF16)
            for one in range(2):
                valued[b][2 * pair + one, :, :TOK] = values[:, one * 128 : one * 128 + 128]
            return
        keys = jnp.dot(lat2[...], kv[i, :, columns], preferred_element_type=F32).astype(BF16)
        for one in range(2):
            rights[b][2 * pair + one, :TOK, :] = keys[:, one * 128 : one * 128 + 128].T
        col = lax.broadcasted_iota(jnp.int32, (TOK, TOK), 1)
        half = col < 64
        low = col % 64 < 32
        t0, t1, t2 = [qv[i, :, pl.ds(pair * 384 + t * 128, 128)] for t in range(3)]
        ropes = jnp.where(half, t1, t2).astype(F32)
        turn = rotated(ropes, cos_v[...], sin_v[...], low).astype(BF16)
        second = pltpu.roll(jnp.where(half, t2, t1).astype(F32), 64, 1).astype(BF16)
        for one, nope in enumerate((t0, second)):
            lefts[b][2 * pair + one, :, :TOK] = nope
            lefts[b][2 * pair + one, :, TOK:] = turn

    def scored(b, h):
        row = lax.broadcasted_iota(jnp.int32, (TOK, TOK), 0)
        col = lax.broadcasted_iota(jnp.int32, (TOK, TOK), 1)
        score = jnp.dot(lefts[b][h], rights[b][h], preferred_element_type=F32)
        score_v[h] = jnp.where(col <= row, score[:, TOK:], score[:, :TOK]) + bias[...]

    def softened(h):
        score = score_v[h]
        top = jnp.max(score, axis=1, keepdims=True)
        weight = jnp.exp2((score - top) * SCALE).astype(BF16)
        prob_v[h, :, :TOK] = weight * up_m[...]
        prob_v[h, :, TOK:] = weight * low_m[...]

    def summed(i, b, h):
        got = jnp.dot(prob_v[h], valued[b][h], preferred_element_type=F32)
        out[:, pl.ds(i * WIDE + h * 128, 128)] = (got[:, :TOK] * (1.0 / got[:, TOK:])).astype(BF16)

    def step(i, b, more=True):
        if b == 0:
            fetched(i + 1)
        elif more:
            pl.when(i + 1 < STEPS)(lambda: fetched(i + 1))
        for h in range(HEADS_STEP + 4):
            if h < HEADS_STEP:
                scored(b, h)
            if 0 <= h - 2 < HEADS_STEP:
                softened(h - 2)
            if 0 <= h - 4 < HEADS_STEP:
                summed(i, b, h - 4)
            if more and 0 <= h - 2 < HEADS_STEP:
                prepare(i + 1, 1 - b, h - 2)

    fetched(0)
    for piece in range(HEADS_STEP):
        prepare(0, 0, piece)

    @pl.loop(0, STEPS // 2 - 1)
    def _(j):
        @pl.when((j == 1) & middle)
        def _():
            done(rs.at[pl.ds(0, 127)], recv1)
            rf[...] = rs[...].astype(F32).reshape(1024, 128)
            pages = jnp.concatenate([rf[pl.ds(t, 256, stride=4), :].astype(BF16) for t in range(4)], axis=1)
            picked = jnp.dot(onehot[...], pages, preferred_element_type=F32)
            for t in range(4):
                for k in range(4):
                    of[pl.ds(t * 4 + k, 128, stride=16), :] = picked[
                        k * 128 : (k + 1) * 128, t * 128 : (t + 1) * 128
                    ]
            os[...] = of[...].reshape(128, 16, 128).astype(BF16)
            cb[my_chunk] = os[me]
            z, x = s // 4, s % 4
            for zh in range(2):
                for xh in range(2):
                    for dg in range(8):
                        a = lax.rem(g + dg, 8)
                        for dz in range(2):
                            for dx in range(2):
                                b = (zh * 2 + lax.rem(z + dz, 2)) * 4 + xh * 2 + lax.rem(x + dx, 2)
                                copy = remote(os.at[a * 16 + b], cb.at[my_chunk], send2, recv2, (a, b))
                                if dg + dz + dx:
                                    copy.start()
                                else:
                                    pl.when((z // 2 != zh) | (x // 2 != xh))(copy.start)

        for b in range(2):
            step(2 * j + b, b)

    step(STEPS - 2, 0)

    @pl.when(middle)
    def _():
        done(cb.at[pl.ds(0, CHUNKS - 1)], recv2)

    @pl.when(jnp.logical_not(middle))
    def _():
        done(cb, recv2)

    cf[...] = cb[...].astype(F32).reshape(CHUNKS * 16, 128)
    half4 = lax.broadcasted_iota(jnp.int32, (4, 128), 1) < 64
    for quad in range(QUADS):
        for two in range(2):
            base = (quad * 2 + two) * 9

            def piece(tile, odd):
                return cf[pl.ds((tile * QUADS + quad) * 16 + (2 * two + odd) * 4, 4), :]

            parts = (
                [piece(tile, 0) for tile in range(4)]
                + [jnp.where(half4, piece(4, 0), piece(0, 1))]
                + [piece(tile, 1) for tile in range(1, 5)]
            )
            for k, part in enumerate(parts):
                cache[:, (base + k) * 128 : (base + k + 1) * 128] = part.astype(BF16)

    step(STEPS - 1, 1, more=False)

    @pl.when(middle)
    def _():
        done(xs.at[pl.ds(0, CHUNKS - 1)], send1)
        done(os.at[pl.ds(0, 127)], send2)

    @pl.when(jnp.logical_not(middle))
    def _():
        done(xs, send1)

    @pl.when(has_right)
    def _():
        lat_copy.wait_send()
        rope_copy.wait_send()


def written(attended, cache, attended_out, cache_out, sem):
    copies = [pltpu.make_async_copy(cache, cache_out, sem.at[4])]
    for i in range(4):
        rows = pl.ds(i * 32, 32)
        copies.append(pltpu.make_async_copy(attended.at[rows], attended_out.at[rows], sem.at[i]))
    for copy in copies:
        copy.start()
    for copy in copies:
        copy.wait()


def on_device(query, latent_raw, rope_raw, kv_gain, w_uk, w_uv, request_lengths, page_owner, page_slot):
    hbm = pl.BlockSpec(memory_space=pltpu.HBM)
    dma = pltpu.SemaphoreType.DMA

    def b16(*shape):
        return pltpu.VMEM(shape, BF16)

    def f32(*shape):
        return pltpu.VMEM(shape, F32)

    vmem = pl.BlockSpec(memory_space=pltpu.VMEM)
    shapes = (
        jax.ShapeDtypeStruct((TOK, HEADS * 128), BF16),
        jax.ShapeDtypeStruct((4, PAGE_W), BF16),
    )
    attended, cache = pl.pallas_call(
        kernel,
        out_shape=(pltpu.VMEM(shapes[0].shape, BF16), pltpu.VMEM(shapes[1].shape, BF16)),
        in_specs=[hbm] * 10,
        out_specs=(vmem, vmem),
        scratch_shapes=[
            pltpu.SMEM((1, 32), jnp.int32),
            f32(1, LATENT),
            b16(TOK, LATENT),
            b16(64, TOK),
            b16(384, 256),
            pltpu.VMEM((1, 256), jnp.int32),
            pltpu.VMEM((1, 256), jnp.int32),
            b16(STEPS, TOK, QWIDE),
            b16(STEPS, LATENT, WIDE),
            b16(STEPS, LATENT, WIDE),
            b16(2 * TOK, LATENT),
            b16(2 * TOK, TOK),
            f32(TOK, TOK),
            f32(TOK, TOK),
            f32(TOK, TOK),
            b16(TOK, TOK),
            b16(TOK, TOK),
            f32(TILES, TOK, 128),
            b16(CHUNKS, 8, 128),
            b16(128, 8, 128),
            f32(1024, 128),
            f32(2048, 128),
            b16(128, 16, 128),
            b16(CHUNKS, 16, 128),
            f32(CHUNKS * 16, 128),
            b16(512, 256),
            b16(HEADS_STEP, TOK, 256),
            b16(HEADS_STEP, TOK, 256),
            b16(HEADS_STEP, 256, 256),
            b16(HEADS_STEP, 256, 256),
            b16(HEADS_STEP, 256, 256),
            b16(HEADS_STEP, 256, 256),
            f32(HEADS_STEP, TOK, TOK),
            b16(HEADS_STEP, TOK, 256),
            dma((7,)),
            dma((STEPS,)),
            dma((STEPS,)),
            dma((STEPS,)),
            dma((2,)),
            dma((2,)),
            dma,
            dma,
            dma,
            dma,
        ],
        compiler_params=pltpu.CompilerParams(
            collective_id=0, has_side_effects=True, vmem_limit_bytes=44 * 2**20
        ),
        name="prefill_and_pages",
    )(
        *(
            pltpu.with_memory_space_constraint(x, pltpu.HBM)
            for x in (
                request_lengths,
                kv_gain.reshape(1, LATENT),
                latent_raw,
                rope_raw.T,
                jnp.asarray(trig_table()),
                page_owner.reshape(1, 256),
                page_slot.reshape(1, 256),
                query,
                w_uk,
                w_uv,
            )
        )
    )
    return pl.pallas_call(
        written,
        out_shape=shapes,
        in_specs=[vmem] * 2,
        out_specs=(hbm, hbm),
        scratch_shapes=[dma((5,))],
        name="results_out",
    )(attended, cache)


def solution(mesh):
    rows = P(("group", "seq"), None)
    return jax.shard_map(
        on_device,
        mesh=mesh,
        in_specs=(rows, rows, rows, P(), P(), P(), P("group", None), P(), P()),
        out_specs=(rows, rows),
        check_vma=False,
    )
```

time: 39.3 us -> 34.3 us (0.87)
  the two profiles are of different devices: /device:TPU:1 before, /device:TPU:32 now
where the time goes in v3:
time: 34.3 us; the launch traced here: 33.8 us
  Pallas kernels  31.1 us (91%)
  local copies, waits for them, and re-layouts  2.07 us (6%)
  between operations  0.65 us (2%)
    pallas_call x1, Pallas kernels, on_device(): pl.pallas_call(kernel, out_shape=(pltpu.VMEM(shapes[0].shape, BF16), pltp...  28.1 us
    pallas_call x1, Pallas kernels, on_device(): pl.pallas_call(written, out_shape=shapes, in_specs=[vmem] * 2, out_specs=...  3.04 us
    unnamed x4, local copies, waits for them, and re-layouts  2.07 us

profile of v3, /device:TPU:32, one launch (start us, length us, event | category | flops | bytes accessed | tf_op | source)
XLA Modules:
  0.0 33.8 jit_solution(9901183579063510518)
XLA Ops:
  0.6 28.1 %prefill_and_pages.1 = (bf16[128,8192]{1,0:T(8,128)(2,1)S(1)}, bf16[4,36864]{1,0:T(4,128)(2,1)S(1)}) custom-call(s32[1,32]{1,0:T(1,128)} %lengths.1, f32[1,512]{1,0:T(1,128)} %bitcast.5, bf16[128,512]{1,0:T(8,128)(2,1)} %latent_raw.1, bf16[64,128]{1,0:T(8,128)(2,1)} %bitcast.4, bf16[384,256]{1,0:T(8,128)(2,1)} %constant.2.clone.trig, s32[1,256]{1,0:T(1,128)} %bitcast.6, ...), custom_call_target="tpu_custom_call" | custom-call | tf_op jit(solution)/shard_map/prefill_and_pages/pallas_call | solution.py:385
  28.7 0.0 copy-start
  28.7 1.3 %copy-done = bf16[128,8192]{1,0:T(8,128)(2,1)} copy-done((bf16[128,8192]{1,0:T(8,128)(2,1)}, bf16[128,8192]{1,0:T(8,128)(2,1)S(1)}, u32[]{:S(2)}) %copy-start) | copy-done | bytes 2097176
  30.1 0.0 copy-start.1
  30.1 0.7 %copy-done.1 = bf16[4,36864]{1,0:T(4,128)(2,1)} copy-done((bf16[4,36864]{1,0:T(4,128)(2,1)}, bf16[4,36864]{1,0:T(4,128)(2,1)S(1)}, u32[]{:S(2)}) %copy-start.1) | copy-done | bytes 294936
  30.8 3.0 %results_out.1 = (bf16[128,8192]{1,0:T(8,128)(2,1)}, bf16[4,36864]{1,0:T(4,128)(2,1)}) custom-call(bf16[128,8192]{1,0:T(8,128)(2,1)} %copy-done, bf16[4,36864]{1,0:T(4,128)(2,1)} %copy-done.1), custom_call_target="tpu_custom_call" | custom-call | tf_op jit(solution)/shard_map/results_out/pallas_call | solution.py:457
Async XLA Ops:
  28.7 1.3 %copy-start = (bf16[128,8192]{1,0:T(8,128)(2,1)}, bf16[128,8192]{1,0:T(8,128)(2,1)S(1)}, u32[]{:S(2)}) copy-start(bf16[128,8192]{1,0:T(8,128)(2,1)S(1)} %get-tuple-element.4.attended) | copy-start | bytes 6291460
  30.1 0.7 %copy-start.1 = (bf16[4,36864]{1,0:T(4,128)(2,1)}, bf16[4,36864]{1,0:T(4,128)(2,1)S(1)}, u32[]{:S(2)}) copy-start(bf16[4,36864]{1,0:T(4,128)(2,1)S(1)} %get-tuple-element.5.cache) | copy-start | bytes 884740

commit v4 on v3

--- a/solution.py
+++ b/solution.py
@@ -461,7 +461,9 @@
         out_specs=(hbm, hbm),
         scratch_shapes=[dma((5,))],
         name="results_out",
-    )(attended, cache)
+    )(
+        pltpu.with_memory_space_constraint(attended, pltpu.VMEM), pltpu.with_memory_space_constraint(cache, pltpu.VMEM)
+    )
 
 
 def solution(mesh):

time: 34.3 us -> 30.6 us (0.89)
  local copies, waits for them, and re-layouts: 2.07 us -> 0 us
  Pallas kernels: 31.1 us -> 29.5 us
    unnamed x4 -> x0, local copies, waits for them, and re-layouts: 2.07 us -> none
    pallas_call x1, Pallas kernels: 3.04 us -> 1.45 us  [on_device(): pl.pallas_call(written, out_shape=shapes, in_specs=[vmem] * 2, out_specs=...]
where the time goes in v4:
time: 30.6 us; the launch traced here: 30.2 us
  Pallas kernels  29.5 us (96%)
  between operations  0.64 us (2%)
    pallas_call x1, Pallas kernels, on_device(): pl.pallas_call(kernel, out_shape=(pltpu.VMEM(shapes[0].shape, BF16), pltp...  28.1 us
    pallas_call x1, Pallas kernels, on_device(): pl.pallas_call(written, out_shape=shapes, in_specs=[vmem] * 2, out_specs=...  1.45 us

profile of v4, /device:TPU:32, one launch (start us, length us, event | category | flops | bytes accessed | tf_op | source)
XLA Modules:
  0.0 30.2 jit_solution(6241037023934063358)
XLA Ops:
  0.6 28.1 %prefill_and_pages.1 = (bf16[128,8192]{1,0:T(8,128)(2,1)S(1)}, bf16[4,36864]{1,0:T(4,128)(2,1)S(1)}) custom-call(s32[1,32]{1,0:T(1,128)} %lengths.1, f32[1,512]{1,0:T(1,128)} %bitcast.5, bf16[128,512]{1,0:T(8,128)(2,1)} %latent_raw.1, bf16[64,128]{1,0:T(8,128)(2,1)} %bitcast.4, bf16[384,256]{1,0:T(8,128)(2,1)} %constant.2.clone.trig, s32[1,256]{1,0:T(1,128)} %bitcast.6, ...), custom_call_target="tpu_custom_call" | custom-call | tf_op jit(solution)/shard_map/prefill_and_pages/pallas_call | solution.py:385
  28.7 1.5 %results_out.1 = (bf16[128,8192]{1,0:T(8,128)(2,1)}, bf16[4,36864]{1,0:T(4,128)(2,1)}) custom-call(bf16[128,8192]{1,0:T(8,128)(2,1)S(1)} %get-tuple-element.4.attended, bf16[4,36864]{1,0:T(4,128)(2,1)S(1)} %get-tuple-element.5.cache), custom_call_target="tpu_custom_call" | custom-call | tf_op jit(solution)/shard_map/results_out/pallas_call | solution.py:457

commit v5 on v4

--- a/solution.py
+++ b/solution.py
@@ -23,6 +23,7 @@
 QWIDE = 1536
 HEADS_STEP = 8
 MIDS = 10
+EVENT = 1
 PAGE_W = 36864
 SCALE = float(1.0 / 192.0**0.5 * np.log2(np.e))
 
@@ -58,9 +59,9 @@
 
 def kernel(
     lengths, gain, latent_raw, rope_raw, trig, owner, slot, query, w_uk, w_uv,
-    out, cache,
+    out, chunks,
     lengths_s, gain_v, latent_v, rope_v, trig_v, owner_v, slot_v,
-    qv, kv, vv, lat2, kr2, cos_v, sin_v, bias, low_m, up_m, ypage, xs, rs, rf, of, os, cb, cf, onehot,
+    qv, kv, vv, lat2, kr2, cos_v, sin_v, bias, low_m, up_m, ypage, xs, rs, rf, of, os, cb, onehot,
     left0, left1, right0, right1, value0, value1, score_v, prob_v,
     in_sem, q_sem, k_sem, v_sem, send_n, recv_n, send1, recv1, send2, recv2,
 ):
@@ -154,7 +155,6 @@
 
     lat_copy = remote(lat2.at[pl.ds(TOK, TOK)], lat2.at[pl.ds(0, TOK)], send_n.at[0], recv_n.at[0], (g, s + 1))
     rope_copy = remote(kr2.at[pl.ds(TOK, TOK)], kr2.at[pl.ds(0, TOK)], send_n.at[1], recv_n.at[1], (g, s + 1))
-    pl.when(has_right & early)(lat_copy.start)
 
     def first_hop(b):
         for a in range(8):
@@ -163,6 +163,9 @@
 
     for b in range(8):
         first_hop(b)
+        rows, there = pl.ds(TOK + 16 * b, 16), pl.ds(16 * b, 16)
+        part = remote(lat2.at[rows], lat2.at[there], send_n.at[0], recv_n.at[0], (g, s + 1))
+        pl.when(has_right & early)(part.start)
 
     for copy in small[2:]:
         copy.wait()
@@ -204,6 +207,35 @@
         want = slot_v[...] * 128 + owner_v[...]
         onehot[...] = (lax.broadcasted_iota(jnp.int32, (512, 256), 0) == want).astype(F32).astype(BF16)
 
+    ahead = s == 4
+    def second_hop():
+        done(rs.at[pl.ds(0, 127)], recv1)
+        rf[...] = rs[...].astype(F32).reshape(1024, 128)
+        pages = jnp.concatenate([rf[pl.ds(t, 256, stride=4), :].astype(BF16) for t in range(4)], axis=1)
+        picked = jnp.dot(onehot[...], pages, preferred_element_type=F32)
+        for t in range(4):
+            for k in range(4):
+                of[pl.ds(t * 4 + k, 128, stride=16), :] = picked[
+                    k * 128 : (k + 1) * 128, t * 128 : (t + 1) * 128
+                ]
+        os[...] = of[...].reshape(128, 16, 128).astype(BF16)
+        cb[my_chunk] = os[me]
+        z, x = s // 4, s % 4
+        for zh in range(2):
+            for xh in range(2):
+                for dg in range(8):
+                    a = lax.rem(g + dg, 8)
+                    for dz in range(2):
+                        for dx in range(2):
+                            b = (zh * 2 + lax.rem(z + dz, 2)) * 4 + xh * 2 + lax.rem(x + dx, 2)
+                            copy = remote(os.at[a * 16 + b], cb.at[my_chunk], send2, recv2, (a, b))
+                            if dg + dz + dx:
+                                copy.start()
+                            else:
+                                pl.when((z // 2 != zh) | (x // 2 != xh))(copy.start)
+
+    pl.when(ahead)(second_hop)
+
     @pl.when(has_left)
     def _():
         done(lat2.at[pl.ds(0, TOK)], recv_n.at[0])
@@ -282,37 +314,14 @@
 
     @pl.loop(0, STEPS // 2 - 1)
     def _(j):
-        @pl.when((j == 1) & middle)
-        def _():
-            done(rs.at[pl.ds(0, 127)], recv1)
-            rf[...] = rs[...].astype(F32).reshape(1024, 128)
-            pages = jnp.concatenate([rf[pl.ds(t, 256, stride=4), :].astype(BF16) for t in range(4)], axis=1)
-            picked = jnp.dot(onehot[...], pages, preferred_element_type=F32)
-            for t in range(4):
-                for k in range(4):
-                    of[pl.ds(t * 4 + k, 128, stride=16), :] = picked[
-                        k * 128 : (k + 1) * 128, t * 128 : (t + 1) * 128
-                    ]
-            os[...] = of[...].reshape(128, 16, 128).astype(BF16)
-            cb[my_chunk] = os[me]
-            z, x = s // 4, s % 4
-            for zh in range(2):
-                for xh in range(2):
-                    for dg in range(8):
-                        a = lax.rem(g + dg, 8)
-                        for dz in range(2):
-                            for dx in range(2):
-                                b = (zh * 2 + lax.rem(z + dz, 2)) * 4 + xh * 2 + lax.rem(x + dx, 2)
-                                copy = remote(os.at[a * 16 + b], cb.at[my_chunk], send2, recv2, (a, b))
-                                if dg + dz + dx:
-                                    copy.start()
-                                else:
-                                    pl.when((z // 2 != zh) | (x // 2 != xh))(copy.start)
-
-        for b in range(2):
-            step(2 * j + b, b)
+        step(2 * j, 0)
+
+        pl.when((j == EVENT // 2) & middle & jnp.logical_not(ahead))(second_hop)
+
+        step(2 * j + 1, 1)
 
     step(STEPS - 2, 0)
+    step(STEPS - 1, 1, more=False)
 
     @pl.when(middle)
     def _():
@@ -322,7 +331,31 @@
     def _():
         done(cb, recv2)
 
-    cf[...] = cb[...].astype(F32).reshape(CHUNKS * 16, 128)
+    chunks[...] = cb[...]
+
+    @pl.when(middle)
+    def _():
+        done(xs.at[pl.ds(0, CHUNKS - 1)], send1)
+        done(os.at[pl.ds(0, 127)], send2)
+
+    @pl.when(jnp.logical_not(middle))
+    def _():
+        done(xs, send1)
+
+    @pl.when(has_right)
+    def _():
+        lat_copy.wait_send()
+        rope_copy.wait_send()
+
+
+def written(attended, chunks, attended_out, cache_out, cf, cache_v, sem):
+    copies = [
+        pltpu.make_async_copy(attended.at[pl.ds(i * 32, 32)], attended_out.at[pl.ds(i * 32, 32)], sem.at[i])
+        for i in range(4)
+    ]
+    for copy in copies:
+        copy.start()
+    cf[...] = chunks[...].astype(F32).reshape(CHUNKS * 16, 128)
     half4 = lax.broadcasted_iota(jnp.int32, (4, 128), 1) < 64
     for quad in range(QUADS):
         for two in range(2):
@@ -337,34 +370,12 @@
                 + [piece(tile, 1) for tile in range(1, 5)]
             )
             for k, part in enumerate(parts):
-                cache[:, (base + k) * 128 : (base + k + 1) * 128] = part.astype(BF16)
-
-    step(STEPS - 1, 1, more=False)
-
-    @pl.when(middle)
-    def _():
-        done(xs.at[pl.ds(0, CHUNKS - 1)], send1)
-        done(os.at[pl.ds(0, 127)], send2)
-
-    @pl.when(jnp.logical_not(middle))
-    def _():
-        done(xs, send1)
-
-    @pl.when(has_right)
-    def _():
-        lat_copy.wait_send()
-        rope_copy.wait_send()
-
-
-def written(attended, cache, attended_out, cache_out, sem):
-    copies = [pltpu.make_async_copy(cache, cache_out, sem.at[4])]
-    for i in range(4):
-        rows = pl.ds(i * 32, 32)
-        copies.append(pltpu.make_async_copy(attended.at[rows], attended_out.at[rows], sem.at[i]))
-    for copy in copies:
-        copy.start()
+                cache_v[:, (base + k) * 128 : (base + k + 1) * 128] = part.astype(BF16)
+    last = pltpu.make_async_copy(cache_v, cache_out, sem.at[4])
+    last.start()
     for copy in copies:
         copy.wait()
+    last.wait()
 
 
 def on_device(query, latent_raw, rope_raw, kv_gain, w_uk, w_uv, request_lengths, page_owner, page_slot):
@@ -382,9 +393,9 @@
         jax.ShapeDtypeStruct((TOK, HEADS * 128), BF16),
         jax.ShapeDtypeStruct((4, PAGE_W), BF16),
     )
-    attended, cache = pl.pallas_call(
+    attended, chunks = pl.pallas_call(
         kernel,
-        out_shape=(pltpu.VMEM(shapes[0].shape, BF16), pltpu.VMEM(shapes[1].shape, BF16)),
+        out_shape=(pltpu.VMEM(shapes[0].shape, BF16), pltpu.VMEM((CHUNKS, 16, 128), BF16)),
         in_specs=[hbm] * 10,
         out_specs=(vmem, vmem),
         scratch_shapes=[
@@ -412,7 +423,6 @@
             f32(2048, 128),
             b16(128, 16, 128),
             b16(CHUNKS, 16, 128),
-            f32(CHUNKS * 16, 128),
             b16(512, 256),
             b16(HEADS_STEP, TOK, 256),
             b16(HEADS_STEP, TOK, 256),
@@ -459,10 +469,10 @@
         out_shape=shapes,
         in_specs=[vmem] * 2,
         out_specs=(hbm, hbm),
-        scratch_shapes=[dma((5,))],
+        scratch_shapes=[f32(CHUNKS * 16, 128), b16(4, PAGE_W), dma((5,))],
         name="results_out",
     )(
-        pltpu.with_memory_space_constraint(attended, pltpu.VMEM), pltpu.with_memory_space_constraint(cache, pltpu.VMEM)
+        pltpu.with_memory_space_constraint(attended, pltpu.VMEM), pltpu.with_memory_space_constraint(chunks, pltpu.VMEM)
     )
 
 

time: 30.6 us -> 29 us (0.948)
  the two profiles are of different devices: /device:TPU:32 before, /device:TPU:5 now
where the time goes in v5:
time: 29 us; the launch traced here: 28.9 us
  Pallas kernels  28.2 us (97%)
  between operations  0.64 us (2%)
    pallas_call x1, Pallas kernels, on_device(): pl.pallas_call(kernel, out_shape=(pltpu.VMEM(shapes[0].shape, BF16), pltp...  26.8 us
    pallas_call x1, Pallas kernels, on_device(): pl.pallas_call(written, out_shape=shapes, in_specs=[vmem] * 2, out_specs=...  1.45 us

profile of v5, /device:TPU:5, one launch (start us, length us, event | category | flops | bytes accessed | tf_op | source)
XLA Modules:
  0.0 28.9 jit_solution(10675262376250898473)
XLA Ops:
  0.6 26.8 %prefill_and_pages.1 = (bf16[128,8192]{1,0:T(8,128)(2,1)S(1)}, bf16[80,16,128]{2,1,0:T(8,128)(2,1)S(1)}) custom-call(s32[1,32]{1,0:T(1,128)} %lengths.1, f32[1,512]{1,0:T(1,128)} %bitcast.5, bf16[128,512]{1,0:T(8,128)(2,1)} %latent_raw.1, bf16[64,128]{1,0:T(8,128)(2,1)} %bitcast.4, bf16[384,256]{1,0:T(8,128)(2,1)} %constant.2.clone.trig, s32[1,256]{1,0:T(1,128)} %bitcast.6, ...), custom_call_target="tpu_custom_call" | custom-call | tf_op jit(solution)/shard_map/prefill_and_pages/pallas_call | solution.py:396
  27.4 1.4 %results_out.1 = (bf16[128,8192]{1,0:T(8,128)(2,1)}, bf16[4,36864]{1,0:T(4,128)(2,1)}) custom-call(bf16[128,8192]{1,0:T(8,128)(2,1)S(1)} %get-tuple-element.4.attended, bf16[80,16,128]{2,1,0:T(8,128)(2,1)S(1)} %get-tuple-element.5.chunks), custom_call_target="tpu_custom_call" | custom-call | tf_op jit(solution)/shard_map/results_out/pallas_call | solution.py:467

commit v6 on v5

--- a/solution.py
+++ b/solution.py
@@ -221,18 +221,23 @@
         os[...] = of[...].reshape(128, 16, 128).astype(BF16)
         cb[my_chunk] = os[me]
         z, x = s // 4, s % 4
+        y = g // 2
+
+        def go(a, c, other):
+            copy = remote(os.at[a * 16 + c], cb.at[my_chunk], send2, recv2, (a, c))
+            if other is None:
+                copy.start()
+            else:
+                pl.when(other)(copy.start)
+
         for zh in range(2):
-            for xh in range(2):
-                for dg in range(8):
-                    a = lax.rem(g + dg, 8)
-                    for dz in range(2):
-                        for dx in range(2):
-                            b = (zh * 2 + lax.rem(z + dz, 2)) * 4 + xh * 2 + lax.rem(x + dx, 2)
-                            copy = remote(os.at[a * 16 + b], cb.at[my_chunk], send2, recv2, (a, b))
-                            if dg + dz + dx:
-                                copy.start()
-                            else:
-                                pl.when((z // 2 != zh) | (x // 2 != xh))(copy.start)
+            for yh in range(2):
+                for dz in range(2):
+                    for dg in range(4):
+                        for dx in range(4):
+                            a = yh * 4 + lax.rem(g + dg, 4)
+                            c = (zh * 2 + lax.rem(z + dz, 2)) * 4 + lax.rem(x + dx, 4)
+                            go(a, c, None if dg + dz + dx else (z // 2 != zh) | (g // 4 != yh))
 
     pl.when(ahead)(second_hop)
 

time: 29 us -> 28.4 us (0.979)
  the two profiles are of different devices: /device:TPU:5 before, /device:TPU:32 now
where the time goes in v6:
time: 28.4 us; the launch traced here: 28.3 us
  Pallas kernels  27.7 us (98%)
  between operations  0.64 us (2%)
    pallas_call x1, Pallas kernels, on_device(): pl.pallas_call(kernel, out_shape=(pltpu.VMEM(shapes[0].shape, BF16), pltp...  26.2 us
    pallas_call x1, Pallas kernels, on_device(): pl.pallas_call(written, out_shape=shapes, in_specs=[vmem] * 2, out_specs=...  1.45 us

profile of v6, /device:TPU:32, one launch (start us, length us, event | category | flops | bytes accessed | tf_op | source)
XLA Modules:
  0.0 28.3 jit_solution(15008221401781571964)
XLA Ops:
  0.6 26.2 %prefill_and_pages.1 = (bf16[128,8192]{1,0:T(8,128)(2,1)S(1)}, bf16[80,16,128]{2,1,0:T(8,128)(2,1)S(1)}) custom-call(s32[1,32]{1,0:T(1,128)} %lengths.1, f32[1,512]{1,0:T(1,128)} %bitcast.5, bf16[128,512]{1,0:T(8,128)(2,1)} %latent_raw.1, bf16[64,128]{1,0:T(8,128)(2,1)} %bitcast.4, bf16[384,256]{1,0:T(8,128)(2,1)} %constant.2.clone.trig, s32[1,256]{1,0:T(1,128)} %bitcast.6, ...), custom_call_target="tpu_custom_call" | custom-call | tf_op jit(solution)/shard_map/prefill_and_pages/pallas_call | solution.py:401
  26.9 1.4 %results_out.1 = (bf16[128,8192]{1,0:T(8,128)(2,1)}, bf16[4,36864]{1,0:T(4,128)(2,1)}) custom-call(bf16[128,8192]{1,0:T(8,128)(2,1)S(1)} %get-tuple-element.4.attended, bf16[80,16,128]{2,1,0:T(8,128)(2,1)S(1)} %get-tuple-element.5.chunks), custom_call_target="tpu_custom_call" | custom-call | tf_op jit(solution)/shard_map/results_out/pallas_call | solution.py:472

commit v7 on v6

--- a/solution.py
+++ b/solution.py
@@ -61,7 +61,7 @@
     lengths, gain, latent_raw, rope_raw, trig, owner, slot, query, w_uk, w_uv,
     out, chunks,
     lengths_s, gain_v, latent_v, rope_v, trig_v, owner_v, slot_v,
-    qv, kv, vv, lat2, kr2, cos_v, sin_v, bias, low_m, up_m, ypage, xs, rs, rf, of, os, cb, onehot,
+    qv, kv, vv, lat2, kr2, krp, cos_v, sin_v, bias, low_m, up_m, ypage, xs, rs, rf, of, os, cb, onehot,
     left0, left1, right0, right1, value0, value1, score_v, prob_v,
     in_sem, q_sem, k_sem, v_sem, send_n, recv_n, send1, recv1, send2, recv2,
 ):
@@ -154,7 +154,7 @@
     pl.semaphore_wait(barrier, 8 * MIDS - jnp.where(middle, 1, 0) + jnp.where(has_right, 1, 0))
 
     lat_copy = remote(lat2.at[pl.ds(TOK, TOK)], lat2.at[pl.ds(0, TOK)], send_n.at[0], recv_n.at[0], (g, s + 1))
-    rope_copy = remote(kr2.at[pl.ds(TOK, TOK)], kr2.at[pl.ds(0, TOK)], send_n.at[1], recv_n.at[1], (g, s + 1))
+    rope_copy = remote(krp.at[pl.ds(64, 64)], krp.at[pl.ds(0, 64)], send_n.at[1], recv_n.at[1], (g, s + 1))
 
     def first_hop(b):
         for a in range(8):
@@ -185,6 +185,7 @@
     key_rope = rotated(rope, cosine, sine, low).astype(BF16)
     kr2[TOK:, :] = key_rope
     tail = key_rope.astype(F32)
+    krp[64:, :] = jnp.where(half[:64], tail[:64], tail[64:]).astype(BF16)
     last_lanes = pltpu.roll(lat2[TOK:, 384:].astype(F32), 64, 1)
     ypage[4] = jnp.where(odd, jnp.where(half, last_lanes, tail), tail)
     chunked(4)
@@ -244,7 +245,11 @@
     @pl.when(has_left)
     def _():
         done(lat2.at[pl.ds(0, TOK)], recv_n.at[0])
-        done(kr2.at[pl.ds(0, TOK)], recv_n.at[1])
+        done(krp.at[pl.ds(0, 64)], recv_n.at[1])
+        packed = krp[:64, :].astype(F32)
+        swapped = pltpu.roll(packed, 64, 1)
+        kr2[:64, :] = jnp.where(half[:64], packed, swapped).astype(BF16)
+        kr2[64:TOK, :] = jnp.where(half[:64], swapped, packed).astype(BF16)
 
     @pl.when(s == 0)
     def _():
@@ -416,6 +421,7 @@
             b16(STEPS, LATENT, WIDE),
             b16(2 * TOK, LATENT),
             b16(2 * TOK, TOK),
+            b16(TOK, TOK),
             f32(TOK, TOK),
             f32(TOK, TOK),
             f32(TOK, TOK),

time: 28.4 us -> 28.2 us (level)
  Pallas kernels: 27.7 us -> 27.3 us
    pallas_call x1, Pallas kernels: 26.2 us -> 25.9 us  [on_device(): pl.pallas_call(kernel, out_shape=(pltpu.VMEM(shapes[0].shape, BF16), pltp...]
where the time goes in v7:
time: 28.2 us; the launch traced here: 28 us
  Pallas kernels  27.3 us (97%)
  between operations  0.64 us (2%)
    pallas_call x1, Pallas kernels, on_device(): pl.pallas_call(kernel, out_shape=(pltpu.VMEM(shapes[0].shape, BF16), pltp...  25.9 us
    pallas_call x1, Pallas kernels, on_device(): pl.pallas_call(written, out_shape=shapes, in_specs=[vmem] * 2, out_specs=...  1.45 us

profile of v7, /device:TPU:32, one launch (start us, length us, event | category | flops | bytes accessed | tf_op | source)
XLA Modules:
  0.0 28.0 jit_solution(3031447739199442417)
XLA Ops:
  0.6 25.9 %prefill_and_pages.1 = (bf16[128,8192]{1,0:T(8,128)(2,1)S(1)}, bf16[80,16,128]{2,1,0:T(8,128)(2,1)S(1)}) custom-call(s32[1,32]{1,0:T(1,128)} %lengths.1, f32[1,512]{1,0:T(1,128)} %bitcast.5, bf16[128,512]{1,0:T(8,128)(2,1)} %latent_raw.1, bf16[64,128]{1,0:T(8,128)(2,1)} %bitcast.4, bf16[384,256]{1,0:T(8,128)(2,1)} %constant.2.clone.trig, s32[1,256]{1,0:T(1,128)} %bitcast.6, ...), custom_call_target="tpu_custom_call" | custom-call | tf_op jit(solution)/shard_map/prefill_and_pages/pallas_call | solution.py:406
  26.5 1.4 %results_out.1 = (bf16[128,8192]{1,0:T(8,128)(2,1)}, bf16[4,36864]{1,0:T(4,128)(2,1)}) custom-call(bf16[128,8192]{1,0:T(8,128)(2,1)S(1)} %get-tuple-element.4.attended, bf16[80,16,128]{2,1,0:T(8,128)(2,1)S(1)} %get-tuple-element.5.chunks), custom_call_target="tpu_custom_call" | custom-call | tf_op jit(solution)/shard_map/results_out/pallas_call | solution.py:478
